TPU v7x, 128 devices: a whole 4x4x4 slice. The times are simulated.
128 devices in a mesh: hid: 8 (over x, core), ep: 16 (over z, y).
Axes of the slice: x: 4, y: 4, z: 4, core: 2. Of those that a mesh axis runs over, the one named last changes fastest.
Arguments:
- gate_proj: bfloat16 [2, 7168, 2048], P(None, 'hid', 'ep'), may hold values from -6 to 6
- up_proj: bfloat16 [2, 7168, 2048], P(None, 'hid', 'ep'), may hold values from -6 to 6
- down_proj: bfloat16 [2, 2048, 7168], P(None, 'ep', 'hid'), may hold values from -6 to 6
- rotation: bfloat16 [7168, 7168], P('hid'), may hold values from -0.0625 to 0.0625
- placement: int32 [2, 16], replicated, may hold values from 0 to 15, each once within a row
- row_count: int32 [2, 16], replicated, may hold values from 16 to 256, as said below
Outputs:
- served: bfloat16 [16, 512, 3, 7168], P('ep', 'hid')
Inputs may be any that keep to these rules, and one draw needn't show every extreme that they name: `row_count`: every count is a multiple of 16, each expert's counts sum to 2048, and one owner holds 256 rows of every expert.
All inputs are finite; a program needn't handle non-finite values.
Results may differ from a plain program's by a relative error of at most 0.017.
Values may be sent and summed in bfloat16 or wider, within the bound.
A program may use at most 128 MiB of HBM per device.

v0:
```python
import jax
import jax.numpy as jnp
from jax import lax
from jax.sharding import PartitionSpec as P


def count_below(bound, residue, shard_total):
    return (bound + shard_total - 1 - residue) // shard_total


def routing(placement, row_count, block_rows):
    owner_total = placement.shape[1]
    blocks = row_count // block_rows
    onehot = (
        placement[:, :, None] == jnp.arange(owner_total, dtype=jnp.int32)[None, None, :]
    ).astype(jnp.int32)
    ordered = jnp.sum(onehot * blocks[:, None, :], axis=2)
    ordered_start = jnp.cumsum(ordered, axis=1) - ordered
    first_block = jnp.sum(onehot * ordered_start[:, :, None], axis=1)
    return (blocks, first_block)


def assemble(received, received_slot, slot_blocks, experts):
    flat_slot = received_slot.reshape(-1)
    matches = flat_slot[None, :] == jnp.arange(slot_blocks, dtype=jnp.int32)[:, None]
    present = jnp.any(matches, axis=1)
    picked = jnp.argmax(matches, axis=1)
    source_ids = picked // experts
    expert_ids = picked % experts
    chosen = received[source_ids, :, expert_ids]
    chosen = jnp.where(present[:, None, None, None], chosen, jnp.zeros((), jnp.bfloat16))
    return chosen.reshape(1, slot_blocks * chosen.shape[1], chosen.shape[2], chosen.shape[3])


def on_device(gate_proj, up_proj, down_proj, rotation, placement, row_count):
    shard_total = lax.axis_size("hid")
    owner_total = lax.axis_size("ep")
    experts, width_part, local_rows = gate_proj.shape
    full_width = rotation.shape[1]
    block_rows = local_rows // shard_total
    stacked = jnp.stack(
        [
            jnp.transpose(gate_proj, (2, 0, 1)),
            jnp.transpose(up_proj, (2, 0, 1)),
            jnp.transpose(down_proj, (1, 0, 2)),
        ],
        axis=2,
    )
    stacked = stacked.reshape(local_rows, experts * 3, width_part)
    summed = lax.psum_scatter(
        jnp.einsum("fck,kh->fch", stacked, rotation, preferred_element_type=jnp.float32).astype(
            jnp.bfloat16
        ),
        "hid",
        scatter_dimension=0,
        tiled=True,
    )
    rotated = summed.reshape(block_rows, experts, 3, full_width)
    shard_here = lax.axis_index("hid")
    owner_here = lax.axis_index("ep")
    block_here = owner_here * shard_total + shard_here
    blocks, first_block = routing(placement, row_count, block_rows)
    inside = ((first_block <= block_here) & (block_here < first_block + blocks)).astype(jnp.int32)
    owner_ids = jnp.arange(owner_total, dtype=jnp.int32)
    target_owner = jnp.sum(inside * owner_ids[None, :], axis=1)
    at_shard = count_below(first_block + blocks, shard_here, shard_total) - count_below(
        first_block, shard_here, shard_total
    )
    offset = jnp.cumsum(at_shard, axis=0) - at_shard
    slot_index = jnp.sum(
        inside * (offset - count_below(first_block, shard_here, shard_total)), axis=1
    )
    slot_index = slot_index + count_below(block_here, shard_here, shard_total)
    slot_blocks = 2 * experts
    all_blocks, all_owner, all_slot = (
        lax.all_gather(rotated[None], "ep", axis=0, tiled=True),
        lax.all_gather(target_owner[None], "ep", axis=0, tiled=True),
        lax.all_gather(slot_index[None], "ep", axis=0, tiled=True),
    )
    received_slot = jnp.where(all_owner == owner_here, all_slot, -1)
    return assemble(all_blocks, received_slot, slot_blocks, experts)


def solution(mesh):
    in_specs = (
        P(None, "hid", "ep"),
        P(None, "hid", "ep"),
        P(None, "ep", "hid"),
        P("hid", None),
        P(),
        P(),
    )
    out_specs = P("ep", "hid", None, None)
    return jax.shard_map(
        on_device, mesh=mesh, in_specs=in_specs, out_specs=out_specs, check_vma=False
    )
```

profile of v0, /device:TPU:0, one launch (start us, length us, event | category | flops | bytes accessed | tf_op | source)
XLA Modules:
  0.0 253.8 jit_solution(16268611063169349019)
XLA Ops:
  6.5 0.0 reduce-scatter.2.cloned.1.call-start
  6.5 1.3 copy.21
  7.8 1.3 copy.22
  9.1 1.2 pad_maximum_fusion
  10.3 0.1 copy.23
  10.4 19.0 %fusion.2 = bf16[128,6,7168]{2,0,1:T(8,128)(2,1)} fusion(bf16[128,6,896]{2,0,1:T(8,128)(2,1)S(1)} %bitcast.22, bf16[896,7168]{1,0:T(8,128)(2,1)} %param.9), kind=kOutput, calls=%fused_computation.3 | convolution fusion | flops 9870508032 | bytes 25231360 | tf_op jit(solution)/shard_map/fck,kh->fch/dot_general | solution.py:51
  29.4 0.0 copy-start
  29.4 0.0 copy-start.1
  29.4 0.0 copy-start.2
  29.4 0.0 reduce-scatter.2.cloned.1.call-update
  29.4 0.0 all-gather.4.cloned.1.call-start
  29.5 67.4 %reduce-scatter.2.cloned.1.call-done = bf16[16,6,7168]{2,0,1:T(8,128)(2,1)} async-done(((bf16[128,6,7168]{2,0,1:T(8,128)(2,1)}), bf16[16,6,7168]{2,0,1:T(8,128)(2,1)}) %reduce-scatter.2.cloned.1.call-update) | async-done | bytes 1376272 | tf_op jit(solution)/shard_map/reduce_scatter | solution.py:50
  96.9 0.0 all-gather.4.cloned.1.call-update
  96.9 0.0 copy-done
  96.9 0.0 copy-done.1
  96.9 0.2 select_reduce_fusion.1
  97.1 0.2 reduce_window_sum.22
  97.3 0.0 copy-done.2
  97.3 0.6 dynamic-slice
  98.6 0.1 select_reduce_fusion
  98.7 0.2 select_reduce_fusion.3
  98.9 0.2 dynamic-update-slice
  99.1 0.1 add_dynamic-update-slice_fusion
  99.2 16.6 %all-reduce.2 = (s32[32]{0:T(128)S(1)}, s32[32]{0:T(128)S(1)}) all-reduce(s32[32]{0:T(128)S(1)} %add_dynamic-update-slice_fusion, s32[32]{0:T(128)S(1)} %dynamic-update-slice), channel_id=3, replica_groups=mesh['hid'=8,'ep'=16] {'ep'}, use_global_device_ids=true, to_apply=%add.1 | all-reduce | flops 64 | bytes 512
  115.8 0.1 fusion.5
  115.9 0.1 broadcast_in_dim.39
  116.0 0.1 broadcast_in_dim.40
  116.1 0.6 iota_reduce_fusion
  116.7 120.2 %all-gather.4.cloned.1.call-done = bf16[16,16,2,3,7168]{4,1,3,2,0:T(8,128)(2,1)} async-done(((bf16[1,16,2,3,7168]{4,1,3,2,0:T(8,128)(2,1)}), bf16[16,16,2,3,7168]{4,1,3,2,0:T(8,128)(2,1)}) %all-gather.4.cloned.1.call-update) | async-done | bytes 22020112 | tf_op jit(solution)/shard_map/all_gather | solution.py:76
  236.9 8.0 %gather_fusion = bf16[4,16,3,7168]{3,1,2,0:T(8,128)(2,1)S(1)} fusion(bf16[16,16,2,3,7168]{4,1,3,2,0:T(8,128)(2,1)} %all-gather.4.cloned.1.call-done, s32[4]{0:T(128)S(1)} %fusion.9), kind=kCustom, calls=%fused_computation | custom fusion | bytes 5505056 | tf_op jit(solution)/shard_map/gather | solution.py:30
  244.9 0.2 copy.24
  245.1 1.9 bitcast_select_fusion
  (8 shorter events, 0.1 us)
Async XLA Ops:
  6.5 90.3 %reduce-scatter.2.cloned.1.call-start = ((), (), s32[]{:S(2)}) async-start(), calls=%async_computation.1 | async-start | bytes 12386304 | tf_op jit(solution)/shard_map/reduce_scatter | solution.py:50
  29.4 67.5 %copy-start = (s32[2,16]{1,0:T(2,128)S(1)}, s32[2,16]{1,0:T(2,128)}, u32[]{:S(2)}) copy-start(s32[2,16]{1,0:T(2,128)} %param.11) | copy-start | bytes 388
  29.4 67.6 %copy-start.1 = (s32[2,16]{1,0:T(2,128)S(1)}, s32[2,16]{1,0:T(2,128)}, u32[]{:S(2)}) copy-start(s32[2,16]{1,0:T(2,128)} %param.10) | copy-start | bytes 388
  29.4 68.0 %copy-start.2 = (u32[128]{0:T(128)S(1)}, u32[128]{0:T(128)}, u32[]{:S(2)}) copy-start(u32[128]{0:T(128)} %constant.126) | copy-start | bytes 1540
  29.4 207.5 %all-gather.4.cloned.1.call-start = ((), (), s32[]{:S(2)}) async-start(), calls=%async_computation.2 | async-start | bytes 23396352 | tf_op jit(solution)/shard_map/all_gather | solution.py:76
Sparse Core Ops, SparseCore 0:
  29.5 67.2 reduce-scatter.1
  99.0 137.8 all-gather.3
where the time goes:
time: 255 us; the launch traced here: 254 us
  waiting for transfers between devices  188 us (74%)
  matrix products  19 us (7%)
  blocking collectives  16.6 us (7%)
  between operations  14.1 us (6%)
  local copies, waits for them, and re-layouts  11.8 us (5%)
  other arithmetic  4.65 us (2%)
    all_gather x1, waiting for transfers between devices, on_device(): lax.all_gather(rotated[None], 'ep', axis=0, tiled=True)  120 us
    reduce_scatter x1, waiting for transfers between devices, on_device(): lax.psum_scatter(jnp.einsum('fck,kh->fch', stacked, rotation, preferred_e...  67.4 us
    dot_general x1, matrix products, on_device(): jnp.einsum('fck,kh->fch', stacked, rotation, preferred_element_type=jnp.f...  19 us
    unnamed x1, blocking collectives  16.6 us
    gather x2, local copies, waits for them, and re-layouts, assemble(): chosen = received[source_ids, :, expert_ids]  8.17 us
  transfers between devices with their start and end apart: 2, of which 2 were waited for; matrix products, arithmetic and copies ran while one was open for 1% of the time, Pallas kernels for 0%

commit v1 on v0

v1 whole, which is shorter than its diff:
```python
import functools

import jax
import jax.numpy as jnp
from jax import lax
from jax.experimental import pallas as pl
from jax.experimental.pallas import tpu as pltpu
from jax.sharding import PartitionSpec as P

MESH = pl.DeviceIdType.MESH
BF = jnp.bfloat16
F32 = jnp.float32
PEERS = (
    (0, 1), (0, 3), (1, 0), (3, 0), (1, 1), (3, 3), (1, 3), (3, 1),
    (0, 2), (2, 0), (1, 2), (2, 1), (3, 2), (2, 3), (2, 2),
)
KINDS = 3
SPLIT = 2
CHUNKS = KINDS * SPLIT
WIDTH = 7168 // SPLIT
QUARTER = WIDTH // 4
TILE = 512


def onehot(rows, cols, condition):
    r = lax.broadcasted_iota(jnp.int32, (rows, cols), 0)
    s = lax.broadcasted_iota(jnp.int32, (rows, cols), 1)
    return jnp.where(condition(r, s), 1.0, 0.0).astype(BF)


def dot(a, b):
    return jnp.dot(a, b, preferred_element_type=F32)


def dot_t(a, b):
    return lax.dot_general(a, b, (((1,), (1,)), ((), ())), preferred_element_type=F32)


def owner_select(h, placement_ref, count_ref):
    owners = lax.broadcasted_iota(jnp.int32, (16, 128), 0)
    low, high = [], []
    for m in range(2):
        start = jnp.int32(0)
        lo = jnp.zeros((16, 128), jnp.int32)
        hi = jnp.zeros((16, 128), jnp.int32)
        for t in range(16):
            o = placement_ref[m, t]
            end = start + lax.shift_right_logical(count_ref[m, o], 4)
            lo = jnp.where(owners == o, lax.shift_right_logical(start + 7 - h, 3), lo)
            hi = jnp.where(owners == o, lax.shift_right_logical(end + 7 - h, 3), hi)
            start = end
        low.append(lo)
        high.append(hi)
    col = lax.broadcasted_iota(jnp.int32, (16, 128), 1)
    m = (col // 16) % 2
    e = col % 16
    lo = jnp.where(m == 0, low[0], low[1])
    hi = jnp.where(m == 0, high[0], high[1])
    slot = e - lo + jnp.where(m == 0, 0, high[0] - low[0])
    slot = jnp.where((lo <= e) & (e < hi), slot, -1)
    slot = jnp.broadcast_to(slot[:, None, :], (16, 16, 128)).reshape(256, 128)
    r = lax.broadcasted_iota(jnp.int32, (256, 128), 0)
    s = lax.broadcasted_iota(jnp.int32, (256, 128), 1)
    keep = (slot == (r // 4) % 4) & (r % 4 == s // 32)
    return jnp.where(keep, 1.0, 0.0).astype(BF)


def kernel(
    placement_ref, count_ref, gate_ref, up_ref, down_ref, rot_hbm, out_hbm,
    rot, src, rcv, lhs, core_out, core_in, own, far_left, far_right, from_left, from_right,
    sel, perm, own_out, own_in, outv,
    rot_sem, src_send, src_recv, core_send, core_recv, x_send, x_recv, own_send, own_recv, out_sem,
):
    hid = lax.axis_index("hid")
    ep = lax.axis_index("ep")
    x, core = hid // 2, hid % 2
    z, y = ep // 4, ep % 4
    right = lax.rem(x + 1, 4) * 2 + core
    left = lax.rem(x + 3, 4) * 2 + core
    other = x * 2 + 1 - core
    peers = [lax.rem(z + dz, 4) * 4 + lax.rem(y + dy, 4) for dz, dy in PEERS]

    barrier = pltpu.get_barrier_semaphore()
    for h in (right, left, other):
        pl.semaphore_signal(barrier, 1, device_id=(h, ep), device_id_type=MESH)
    for p in peers:
        pl.semaphore_signal(barrier, 1, device_id=(hid, p), device_id_type=MESH)

    rot_copy = pltpu.make_async_copy(rot_hbm, rot, rot_sem)
    rot_copy.start()

    spread = [
        onehot(256, 128, lambda r, s: ((r // 8) % 2 == m) & (s == (r % 8) * 16 + r // 16))
        for m in range(2)
    ]
    for k, ref in enumerate((gate_ref, up_ref)):
        rows = dot_t(spread[0], ref[0]) + dot_t(spread[1], ref[1])
        src[k] = rows.astype(BF).reshape(16, 16, 896)
    rows = dot(spread[0], down_ref[0]) + dot(spread[1], down_ref[1])
    src[2] = rows.astype(BF).reshape(16, 16, 896)

    pl.semaphore_wait(barrier, 3 + len(PEERS))

    def src_copy(k, i):
        return pltpu.make_async_remote_copy(
            src.at[k, peers[i]], rcv.at[k, ep], src_send.at[k, i], src_recv.at[k, i],
            device_id=(hid, peers[i]), device_id_type=MESH,
        )

    for k in range(KINDS):
        for i in range(len(PEERS)):
            src_copy(k, i).start()
    for k in range(KINDS):
        rcv[k, ep] = src[k, ep]

    sel[...] = owner_select(hid, placement_ref, count_ref)

    def arrange(r, s):
        d = (r // 32) % 4
        d = jnp.where(d == 0, 2, jnp.where(d == 1, 1, jnp.where(d == 2, 3, 0)))
        b = ((x + d) % 4) * 2 + jnp.where(r < 128, 1 - core, core)
        return s == (r % 16) * 16 + ((r // 16) % 2) * 8 + b

    perm[0] = onehot(256, 256, arrange)
    perm[1] = onehot(
        256, 256, lambda r, s: s == (r % 16) * 16 + ((r // 16) % 4) * 4 + r // 64
    )

    def core_copy(n):
        return pltpu.make_async_remote_copy(
            core_out.at[n], core_in.at[n], core_send.at[n], core_recv.at[n],
            device_id=(other, ep), device_id_type=MESH,
        )

    def x_copy(n, i):
        first, to, dst = (
            (0, right, far_left.at[n]),
            (16, left, far_right.at[n]),
            (48, right, from_left.at[n, pl.ds(16, 16)]),
            (64, left, from_right.at[n, pl.ds(0, 16)]),
            (32, right, from_left.at[n, pl.ds(0, 16)]),
            (80, left, from_right.at[n, pl.ds(16, 16)]),
        )[i]
        return pltpu.make_async_remote_copy(
            own.at[n, pl.ds(first, 16)], dst, x_send.at[n, i], x_recv.at[n, i],
            device_id=(to, ep), device_id_type=MESH,
        )

    def own_copy(n, i):
        return pltpu.make_async_remote_copy(
            own_out.at[n, peers[i]], own_in.at[n, ep], own_send.at[n, i], own_recv.at[n, i],
            device_id=(hid, peers[i]), device_id_type=MESH,
        )

    def out_copy(n):
        columns = pl.ds(pl.multiple_of((n % SPLIT) * WIDTH, 128), WIDTH)
        return pltpu.make_async_copy(outv.at[n], out_hbm.at[n // SPLIT, :, columns], out_sem.at[n])

    def add(n, first, rows, ref):
        own[n, first:first + rows] = (
            own[n, first:first + rows].astype(F32) + ref.astype(F32)
        ).astype(BF)

    def multiply(n):
        k = n // SPLIT

        @pl.when(n % SPLIT == 0)
        def _():
            for i in range(len(PEERS)):
                src_copy(k, i).wait_recv()
            lhs[k] = dot(perm[0], rcv[k].reshape(256, 896)).astype(BF)

        @pl.loop(0, WIDTH // TILE)
        def _(t):
            here = pl.ds(pl.multiple_of(t * TILE, TILE), TILE)
            there = pl.ds(pl.multiple_of((n % SPLIT) * WIDTH + t * TILE, TILE), TILE)
            total = dot(lhs[k], rot[:, there])
            core_out[n, :, here] = total[:128].astype(BF)
            own[n, :, here] = total[128:].astype(BF)

        core_copy(n).start()

    def sum_cores(n):
        core_copy(n).wait_recv()
        add(n, 0, 32, core_in[n, 0:32])
        x_copy(n, 0).start()
        x_copy(n, 1).start()
        add(n, 32, 64, core_in[n, 32:96])
        x_copy(n, 2).start()
        x_copy(n, 3).start()
        add(n, 96, 32, core_in[n, 96:128])

    def pass_on(n):
        x_copy(n, 0).wait_recv()
        add(n, 32, 16, far_left[n])
        x_copy(n, 4).start()
        x_copy(n, 1).wait_recv()
        add(n, 80, 16, far_right[n])
        x_copy(n, 5).start()

    def to_owners(n):
        for i in range(2, 6):
            x_copy(n, i).wait_recv()
        parts = []
        for g in range(4):
            at = slice(g * QUARTER, (g + 1) * QUARTER)
            parts.append((
                own[n, 96:128, at].astype(F32)
                + from_left[n, :, at].astype(F32)
                + from_right[n, :, at].astype(F32)
            ).astype(BF))
        rows = dot(sel[...], jnp.concatenate(parts, axis=0))
        own_out[n] = rows.astype(BF).reshape(16, 16, QUARTER)
        for i in range(len(PEERS)):
            own_copy(n, i).start()
        own_in[n, ep] = own_out[n, ep]

    def place(n):
        for i in range(len(PEERS)):
            own_copy(n, i).wait_recv()
        rows = dot(perm[1], own_in[n].reshape(256, QUARTER)).astype(BF)
        for g in range(4):
            outv[n, :, g * QUARTER:(g + 1) * QUARTER] = rows[g * 64:(g + 1) * 64]
        out_copy(n).start()

    rot_copy.wait()

    stages = (multiply, sum_cores, pass_on, to_owners, place)
    lags = (0, 1, 2, 3, 4)

    @pl.loop(0, CHUNKS + lags[-1])
    def _(t):
        for stage, lag in zip(stages, lags):
            @pl.when((t >= lag) & (t < CHUNKS + lag))
            def _():
                stage(t - lag)

    for k in range(KINDS):
        for i in range(len(PEERS)):
            src_copy(k, i).wait_send()

    @pl.loop(0, CHUNKS)
    def _(n):
        core_copy(n).wait_send()
        for i in range(6):
            x_copy(n, i).wait_send()
        for i in range(len(PEERS)):
            own_copy(n, i).wait_send()
        out_copy(n).wait()


def on_device(gate_proj, up_proj, down_proj, rotation, placement, row_count):
    dma = pltpu.SemaphoreType.DMA
    peers = len(PEERS)
    vmem = pl.BlockSpec(memory_space=pltpu.VMEM)
    smem = pl.BlockSpec(memory_space=pltpu.SMEM)
    hbm = pl.BlockSpec(memory_space=pl.ANY)
    out = pl.pallas_call(
        kernel,
        out_shape=jax.ShapeDtypeStruct((3, 64, 7168), BF),
        in_specs=[smem, smem, vmem, vmem, vmem, hbm],
        out_specs=hbm,
        scratch_shapes=[
            pltpu.VMEM((896, 7168), BF),
            pltpu.VMEM((KINDS, 16, 16, 896), BF),
            pltpu.VMEM((KINDS, 16, 16, 896), BF),
            pltpu.VMEM((KINDS, 256, 896), BF),
            pltpu.VMEM((CHUNKS, 128, WIDTH), BF),
            pltpu.VMEM((CHUNKS, 128, WIDTH), BF),
            pltpu.VMEM((CHUNKS, 128, WIDTH), BF),
            pltpu.VMEM((CHUNKS, 16, WIDTH), BF),
            pltpu.VMEM((CHUNKS, 16, WIDTH), BF),
            pltpu.VMEM((CHUNKS, 32, WIDTH), BF),
            pltpu.VMEM((CHUNKS, 32, WIDTH), BF),
            pltpu.VMEM((256, 128), BF),
            pltpu.VMEM((2, 256, 256), BF),
            pltpu.VMEM((CHUNKS, 16, 16, QUARTER), BF),
            pltpu.VMEM((CHUNKS, 16, 16, QUARTER), BF),
            pltpu.VMEM((CHUNKS, 64, WIDTH), BF),
            dma,
            dma((KINDS, peers)),
            dma((KINDS, peers)),
            dma((CHUNKS,)),
            dma((CHUNKS,)),
            dma((CHUNKS, 6)),
            dma((CHUNKS, 6)),
            dma((CHUNKS, peers)),
            dma((CHUNKS, peers)),
            dma((CHUNKS,)),
        ],
        compiler_params=pltpu.CompilerParams(
            collective_id=0, has_side_effects=True, vmem_limit_bytes=60 * 1024 * 1024
        ),
        name="rotate_and_place",
    )(placement, row_count, gate_proj, up_proj, down_proj, rotation)
    return jnp.transpose(out, (1, 0, 2))[None]


def solution(mesh):
    in_specs = (
        P(None, "hid", "ep"),
        P(None, "hid", "ep"),
        P(None, "ep", "hid"),
        P("hid", None),
        P(),
        P(),
    )
    out_specs = P("ep", "hid", None, None)
    return jax.shard_map(
        on_device, mesh=mesh, in_specs=in_specs, out_specs=out_specs, check_vma=False
    )
```

time: 255 us -> 90.3 us (0.35)
  waiting for transfers between devices: 188 us -> 0 us
  Pallas kernels: 0 us -> 86.7 us
  matrix products: 19 us -> 0 us
  blocking collectives: 16.6 us -> 0 us
  between operations: 14.1 us -> 0.01 us
  local copies, waits for them, and re-layouts: 11.8 us -> 3.49 us
  other arithmetic: 4.65 us -> 0 us
    all_gather x1 -> x0, waiting for transfers between devices: 120 us -> none  [on_device(): lax.all_gather(rotated[None], 'ep', axis=0, tiled=True)]
    pallas_call x0 -> x1, Pallas kernels: none -> 86.7 us  [on_device(): pl.pallas_call(kernel, out_shape=jax.ShapeDtypeStruct((3, 64, 7168), BF),...]
    reduce_scatter x1 -> x0, waiting for transfers between devices: 67.4 us -> none  [on_device(): lax.psum_scatter(jnp.einsum('fck,kh->fch', stacked, rotation, preferred_e...]
    dot_general x1 -> x0, matrix products: 19 us -> none  [on_device(): jnp.einsum('fck,kh->fch', stacked, rotation, preferred_element_type=jnp.f...]
    unnamed x1 -> x0, blocking collectives: 16.6 us -> none
    gather x2 -> x0, local copies, waits for them, and re-layouts: 8.17 us -> none  [assemble(): chosen = received[source_ids, :, expert_ids]]
  transfers between devices with their start and end apart: 2 -> 0, of which waited for: 2 -> 0; matrix products, arithmetic and copies ran while one was open for 1% -> 0% of each run, Pallas kernels for 0% -> 0%
where the time goes in v1:
time: 90.3 us; the launch traced here: 90.2 us
  Pallas kernels  86.7 us (96%)
  local copies, waits for them, and re-layouts  3.49 us (4%)
    pallas_call x1, Pallas kernels, on_device(): pl.pallas_call(kernel, out_shape=jax.ShapeDtypeStruct((3, 64, 7168), BF),...  86.7 us
    unnamed x1, local copies, waits for them, and re-layouts  3.49 us

profile of v1, /device:TPU:0, one launch (start us, length us, event | category | flops | bytes accessed | tf_op | source)
XLA Modules:
  0.0 90.2 jit_solution(7513997366213272037)
XLA Ops:
  0.0 86.7 %rotate_and_place.1 = bf16[3,64,7168]{2,1,0:T(8,128)(2,1)} custom-call(s32[2,16]{1,0:T(2,128)} %placement_ref.1, s32[2,16]{1,0:T(2,128)} %count_ref.1, bf16[2,896,128]{2,1,0:T(8,128)(2,1)} %gate_ref.1, bf16[2,896,128]{2,1,0:T(8,128)(2,1)} %up_ref.1, bf16[2,128,896]{2,1,0:T(8,128)(2,1)} %down_ref.1, bf16[896,7168]{1,0:T(8,128)(2,1)} %rot_hbm.1), custom_call_target="tpu_custom_call" | custom-call | tf_op jit(solution)/shard_map/rotate_and_place/pallas_call | solution.py:258
  86.7 3.5 %copy.8 = bf16[1,64,3,7168]{3,1,2,0:T(8,128)(2,1)} copy(bf16[1,64,3,7168]{3,1,2,0:T(8,128)(2,1)} %bitcast.3) | data formatting | bytes 5505024

commit v2 on v0

v2 whole, which is shorter than its diff:
```python
import jax
import jax.numpy as jnp
from jax import lax
from jax.experimental import pallas as pl
from jax.experimental.pallas import tpu as pltpu
from jax.sharding import PartitionSpec as P

MESH = pl.DeviceIdType.MESH
BF = jnp.bfloat16
F32 = jnp.float32
PEERS = (
    (0, 1), (0, 3), (1, 0), (3, 0), (1, 1), (3, 3), (1, 3), (3, 1),
    (0, 2), (2, 0), (1, 2), (2, 1), (3, 2), (2, 3), (2, 2),
)
OTHERS = len(PEERS)
HIDDEN = 7168
PIECE = 896
A_WIDTHS = (1024, 2048, 4096)
A_STARTS = (0, 1024, 3072)
A_CHUNKS = len(A_WIDTHS)
B_WIDTH = 1024
B_CHUNKS = HIDDEN // B_WIDTH
B_QUARTER = B_WIDTH // 4
TILE = 1024


def iotas(rows, cols):
    return (
        lax.broadcasted_iota(jnp.int32, (rows, cols), 0),
        lax.broadcasted_iota(jnp.int32, (rows, cols), 1),
    )


def onehot(condition):
    return jnp.where(condition, 1.0, 0.0).astype(BF)


def dot(a, b):
    return jnp.dot(a, b, preferred_element_type=F32)


def dot_t(a, b):
    return lax.dot_general(a, b, (((1,), (1,)), ((), ())), preferred_element_type=F32)


def ring_offset(index):
    return jnp.where(index == 0, 2, jnp.where(index == 1, 1, jnp.where(index == 2, 3, 0)))


def ranges(h, ep, placement_ref, count_ref):
    owners, _ = iotas(16, 256)
    low, high, mine = [], [], []
    for m in range(2):
        start = jnp.int32(0)
        count = jnp.int32(0)
        lo = jnp.zeros((16, 256), jnp.int32)
        hi = jnp.zeros((16, 256), jnp.int32)
        for t in range(16):
            o = placement_ref[m, t]
            end = start + lax.shift_right_logical(count_ref[m, o], 4)
            first = lax.shift_right_logical(start + 7 - h, 3)
            last = lax.shift_right_logical(end + 7 - h, 3)
            lo = jnp.where(owners == o, first, lo)
            hi = jnp.where(owners == o, last, hi)
            count = jnp.where(o == ep, last - first, count)
            start = end
        low.append(lo)
        high.append(hi)
        mine.append(count)
    return low, high, mine


def select_a(ep, low, high):
    first = ep < 8
    lo = jnp.where(first, low[0], low[1])
    hi = jnp.where(first, high[0], high[1])
    _, col = iotas(16, 256)
    e = col // 16
    place = jnp.where((lo <= e) & (e < hi), e - lo, -1)
    place = jnp.broadcast_to(place[:, None, :], (16, 32, 256)).reshape(512, 256)
    r, s = iotas(512, 256)
    return onehot((place == (r // 16) % 2) & (r % 16 == s % 16))


def place_a(mine):
    r, s = iotas(64, 64)
    slot = (s // 16) % 2 + jnp.where(s < 32, 0, mine[0])
    return onehot((slot == r // 16) & (r % 16 == s % 16))


def select_b(low, high):
    _, col = iotas(16, 128)
    m = (col // 16) % 2
    e = col % 16
    low = [v[:, :128] for v in low]
    high = [v[:, :128] for v in high]
    lo = jnp.where(m == 0, low[0], low[1])
    hi = jnp.where(m == 0, high[0], high[1])
    slot = e - lo + jnp.where(m == 0, 0, high[0] - low[0])
    slot = jnp.where((lo <= e) & (e < hi), slot, -1)
    slot = jnp.broadcast_to(slot[:, None, :], (16, 16, 128)).reshape(256, 128)
    r, s = iotas(256, 128)
    return onehot((slot == (r // 4) % 4) & (r % 4 == s // 32))


def kernel(
    placement_ref, count_ref, gate_ref, up_ref, down_ref, rot_hbm, out_hbm, *scratch
):
    scratch = list(scratch)

    def take(count):
        taken = scratch[:count]
        del scratch[:count]
        return taken

    rot, lhs_a, lhs_b, src, rcv, sel_a, put_a, sel_b, put_b, arrange = take(10)
    a_core_out, a_core_in, a_own, a_far, a_from, a_sum, a_in, a_pick, a_got, a_out = (
        take(A_CHUNKS) for _ in range(10)
    )
    b_core_out, b_core_in, b_own, b_far, b_from, b_pick, b_got, b_out = take(8)
    rot_sem, src_send, src_recv = take(3)
    a_core_send, a_core_recv, a_x_send, a_x_recv, a_in_send, a_in_recv = take(6)
    a_own_send, a_own_recv, a_out_sem = take(3)
    b_core_send, b_core_recv, b_x_send, b_x_recv, b_own_send, b_own_recv, b_out_sem = take(7)

    hid = lax.axis_index("hid")
    ep = lax.axis_index("ep")
    x, core = hid // 2, hid % 2
    z, y = ep // 4, ep % 4
    right = lax.rem(x + 1, 4) * 2 + core
    left = lax.rem(x + 3, 4) * 2 + core
    other = x * 2 + 1 - core
    peers = [lax.rem(z + dz, 4) * 4 + lax.rem(y + dy, 4) for dz, dy in PEERS]

    def remote(source, target, send, recv, h, e):
        return pltpu.make_async_remote_copy(
            source, target, send, recv, device_id=(h, e), device_id_type=MESH
        )

    barrier = pltpu.get_barrier_semaphore()
    for h in (right, left, other):
        pl.semaphore_signal(barrier, 1, device_id=(h, ep), device_id_type=MESH)
    for p in peers:
        pl.semaphore_signal(barrier, 1, device_id=(hid, p), device_id_type=MESH)

    def rot_copy(c):
        columns = pl.ds(A_STARTS[c], A_WIDTHS[c])
        return pltpu.make_async_copy(rot_hbm.at[:, columns], rot.at[:, columns], rot_sem.at[c])

    def src_copy(k, i):
        return remote(
            src.at[k, peers[i]], rcv.at[k, ep], src_send.at[k, i], src_recv.at[k, i], hid, peers[i]
        )

    def x_copy(own, far, near, send, recv, half, i):
        first, to, target = (
            (0, right, far.at[0]),
            (1, left, far.at[1]),
            (3, right, near.at[0, pl.ds(half, half)]),
            (4, left, near.at[1, pl.ds(0, half)]),
            (2, right, near.at[0, pl.ds(0, half)]),
            (5, left, near.at[1, pl.ds(half, half)]),
        )[i]
        return remote(own.at[pl.ds(first * half, half)], target, send.at[i], recv.at[i], to, ep)

    def a_x(c, i):
        return x_copy(a_own[c], a_far[c], a_from[c], a_x_send.at[c], a_x_recv.at[c], 16, i)

    def b_x(n, i):
        return x_copy(
            b_own.at[n], b_far.at[n], b_from.at[n], b_x_send.at[n], b_x_recv.at[n], 32, i
        )

    def a_core(c):
        return remote(a_core_out[c], a_core_in[c], a_core_send.at[c], a_core_recv.at[c], other, ep)

    def b_core(n):
        return remote(
            b_core_out.at[n], b_core_in.at[n], b_core_send.at[n], b_core_recv.at[n], other, ep
        )

    def a_spread(c, i):
        return remote(
            a_sum[c].at[peers[i]], a_in[c].at[ep], a_in_send.at[c, i], a_in_recv.at[c, i],
            hid, peers[i],
        )

    def a_owner(c, i):
        return remote(
            a_pick[c].at[peers[i]], a_got[c].at[ep], a_own_send.at[c, i], a_own_recv.at[c, i],
            hid, peers[i],
        )

    def b_owner(n, i):
        return remote(
            b_pick.at[n, peers[i]], b_got.at[n, ep], b_own_send.at[n, i], b_own_recv.at[n, i],
            hid, peers[i],
        )

    def a_store(c):
        columns = pl.ds(A_STARTS[c], A_WIDTHS[c])
        return pltpu.make_async_copy(a_out[c], out_hbm.at[0, :, columns], a_out_sem.at[c])

    def b_store(n):
        columns = pl.ds(pl.multiple_of(n * B_WIDTH, B_WIDTH), B_WIDTH)
        return pltpu.make_async_copy(
            b_out.at[n], out_hbm.at[pl.ds(1, 2), :, columns], b_out_sem.at[n]
        )

    def sum_cores(own, core_in, half, start_x):
        own[0:2 * half] += core_in[0:2 * half]
        start_x(0)
        start_x(1)
        own[2 * half:6 * half] += core_in[2 * half:6 * half]
        start_x(2)
        start_x(3)
        own[6 * half:8 * half] += core_in[6 * half:8 * half]

    def pass_on(own, far, half, x_of):
        x_of(0).wait_recv()
        own[2 * half:3 * half] += far[0]
        x_of(4).start()
        x_of(1).wait_recv()
        own[5 * half:6 * half] += far[1]
        x_of(5).start()

    def total_of(own, near, half, rows, columns):
        return (
            own[6 * half + rows.start:6 * half + rows.stop, columns].astype(F32)
            + near[0, rows, columns].astype(F32)
            + near[1, rows, columns].astype(F32)
        ).astype(BF)

    def a_multiply(c):
        rot_copy(c).wait()

        @pl.loop(0, A_WIDTHS[c] // TILE)
        def _(t):
            here = pl.ds(pl.multiple_of(t * TILE, TILE), TILE)
            there = pl.ds(pl.multiple_of(A_STARTS[c] + t * TILE, TILE), TILE)
            total = dot(lhs_a[...], rot[:, there])
            a_core_out[c][:, here] = total[:128].astype(BF)
            a_own[c][:, here] = total[128:].astype(BF)

    def a_sum_cores(c):
        a_core(c).wait_recv()
        sum_cores(a_own[c], a_core_in[c], 16, lambda i: a_x(c, i).start())

    def a_pass_on(c):
        pass_on(a_own[c], a_far[c], 16, lambda i: a_x(c, i))

    def a_to_peers(c):
        for i in range(2, 6):
            a_x(c, i).wait_recv()
        eighth = A_WIDTHS[c] // 8
        for m in range(2):
            for q in range(8):
                a_sum[c][m * 8 + q] = total_of(
                    a_own[c], a_from[c], 16,
                    slice(m * 16, m * 16 + 16), slice(q * eighth, (q + 1) * eighth),
                )
        for i in range(OTHERS):
            a_spread(c, i).start()
        a_in[c][ep] = a_sum[c][ep]

    def a_to_owners(c):
        for i in range(OTHERS):
            a_spread(c, i).wait_recv()
        eighth = A_WIDTHS[c] // 8
        rows = dot(sel_a[...], a_in[c][...].reshape(256, eighth))
        a_pick[c][...] = rows.astype(BF).reshape(16, 32, eighth)
        for i in range(OTHERS):
            a_owner(c, i).start()
        a_got[c][ep] = a_pick[c][ep]

    def a_place(c):
        for i in range(OTHERS):
            a_owner(c, i).wait_recv()
        eighth = A_WIDTHS[c] // 8
        for q in range(8):
            both = jnp.concatenate([a_got[c][q], a_got[c][8 + q]], axis=0)
            a_out[c][:, q * eighth:(q + 1) * eighth] = dot(put_a[...], both).astype(BF)
        a_store(c).start()

    def b_multiply(n):
        here = pl.ds(pl.multiple_of(n * B_WIDTH, B_WIDTH), B_WIDTH)
        total = dot(lhs_b[...], rot[:, here])
        b_core_out[n] = total[:256].astype(BF)
        b_own[n] = total[256:].astype(BF)
        b_core(n).start()

    def b_sum_cores(n):
        b_core(n).wait_recv()
        sum_cores(b_own.at[n], b_core_in.at[n], 32, lambda i: b_x(n, i).start())

    def b_pass_on(n):
        pass_on(b_own.at[n], b_far.at[n], 32, lambda i: b_x(n, i))

    def b_to_owners(n):
        for i in range(2, 6):
            b_x(n, i).wait_recv()
        quarters = []
        for g in range(4):
            columns = slice(g * B_QUARTER, (g + 1) * B_QUARTER)
            quarters.append(jnp.concatenate([
                total_of(b_own.at[n], b_from.at[n], 32, slice(k * 32, k * 32 + 32), columns)
                for k in range(2)
            ], axis=1))
        rows = dot(sel_b[...], jnp.concatenate(quarters, axis=0))
        b_pick[n] = rows.astype(BF).reshape(16, 16, 2 * B_QUARTER)
        for i in range(OTHERS):
            b_owner(n, i).start()
        b_got[n, ep] = b_pick[n, ep]

    def b_place(n):
        for i in range(OTHERS):
            b_owner(n, i).wait_recv()
        rows = dot(put_b[...], b_got[n].reshape(256, 2 * B_QUARTER)).astype(BF)
        for k in range(2):
            for g in range(4):
                b_out[n, k, :, g * B_QUARTER:(g + 1) * B_QUARTER] = rows[
                    g * 64:(g + 1) * 64, k * B_QUARTER:(k + 1) * B_QUARTER
                ]
        b_store(n).start()

    for c in range(A_CHUNKS):
        rot_copy(c).start()

    r, s = iotas(256, 128)
    block = ((x + ring_offset((r // 32) % 4)) % 4) * 2 + jnp.where(r < 128, 1 - core, core)
    column = block * 16 + r % 16
    expert = (r // 16) % 2
    rows = sum(dot_t(onehot((expert == m) & (s == column)), gate_ref[m]) for m in range(2))
    lhs_a[...] = rows.astype(BF)

    column = (r % 8) * 16 + r // 16
    expert = (r // 8) % 2
    spread = [onehot((expert == m) & (s == column)) for m in range(2)]
    rows = sum(dot_t(spread[m], up_ref[m]) for m in range(2))
    src[0] = rows.astype(BF).reshape(16, 16, PIECE)
    rows = sum(dot(spread[m], down_ref[m]) for m in range(2))
    src[1] = rows.astype(BF).reshape(16, 16, PIECE)
    for k in range(2):
        rcv[k, ep] = src[k, ep]

    for c in range(A_CHUNKS):
        a_multiply(c)

    low, high, mine = ranges(hid, ep, placement_ref, count_ref)
    sel_a[...] = select_a(ep, low, high)
    put_a[...] = place_a(mine)
    sel_b[...] = select_b(low, high)
    r, s = iotas(256, 256)
    put_b[...] = onehot(s == (r % 16) * 16 + ((r // 16) % 4) * 4 + r // 64)
    r, s = iotas(512, 512)
    block = ((x + ring_offset((r // 64) % 4)) % 4) * 2 + jnp.where(r < 256, 1 - core, core)
    arrange[...] = onehot(
        s == ((r // 32) % 2) * 256 + (r % 16) * 16 + ((r // 16) % 2) * 8 + block
    )

    pl.semaphore_wait(barrier, 3 + OTHERS)

    for c in range(A_CHUNKS):
        a_core(c).start()
    for i in range(OTHERS):
        src_copy(0, i).start()
    a_sum_cores(0)
    for i in range(OTHERS):
        src_copy(1, i).start()
    a_sum_cores(1)
    a_pass_on(0)
    a_sum_cores(2)
    a_pass_on(1)
    a_to_peers(0)
    a_pass_on(2)

    for k in range(2):
        for i in range(OTHERS):
            src_copy(k, i).wait_recv()
    lhs_b[...] = dot(arrange[...], rcv[...].reshape(512, PIECE)).astype(BF)
    b_multiply(0)
    a_to_peers(1)

    stages = ((b_sum_cores, 0), (b_multiply, -1), (b_pass_on, 1), (b_to_owners, 2), (b_place, 3))
    extras = {
        0: (lambda: a_to_owners(0), lambda: a_to_peers(2)),
        1: (lambda: a_to_owners(1),),
        2: (lambda: a_to_owners(2), lambda: a_place(0), lambda: a_place(1)),
        3: (lambda: a_place(2),),
    }

    @pl.loop(0, B_CHUNKS + 3)
    def _(t):
        for stage, lag in stages:
            @pl.when((t >= lag) & (t < B_CHUNKS + lag))
            def _():
                stage(t - lag)
        for at, work in extras.items():
            @pl.when(t == at)
            def _():
                for one in work:
                    one()

    for k in range(2):
        for i in range(OTHERS):
            src_copy(k, i).wait_send()
    for c in range(A_CHUNKS):
        a_core(c).wait_send()
        for i in range(6):
            a_x(c, i).wait_send()
        for i in range(OTHERS):
            a_spread(c, i).wait_send()
            a_owner(c, i).wait_send()
        a_store(c).wait()

    @pl.loop(0, B_CHUNKS)
    def _(n):
        b_core(n).wait_send()
        for i in range(6):
            b_x(n, i).wait_send()
        for i in range(OTHERS):
            b_owner(n, i).wait_send()
        b_store(n).wait()


def on_device(gate_proj, up_proj, down_proj, rotation, placement, row_count):
    dma = pltpu.SemaphoreType.DMA
    vmem = pl.BlockSpec(memory_space=pltpu.VMEM)
    smem = pl.BlockSpec(memory_space=pltpu.SMEM)
    hbm = pl.BlockSpec(memory_space=pl.ANY)

    def held(*shape):
        return pltpu.VMEM(shape, BF)

    def per_a(shape_of):
        return [held(*shape_of(w)) for w in A_WIDTHS]

    b = B_CHUNKS
    scratch = [
        held(PIECE, HIDDEN), held(256, PIECE), held(512, PIECE),
        held(2, 16, 16, PIECE), held(2, 16, 16, PIECE),
        held(512, 256), held(64, 64), held(256, 128), held(256, 256), held(512, 512),
        *per_a(lambda w: (128, w)),
        *per_a(lambda w: (128, w)),
        *per_a(lambda w: (128, w)),
        *per_a(lambda w: (2, 16, w)),
        *per_a(lambda w: (2, 32, w)),
        *per_a(lambda w: (16, 16, w // 8)),
        *per_a(lambda w: (16, 16, w // 8)),
        *per_a(lambda w: (16, 32, w // 8)),
        *per_a(lambda w: (16, 32, w // 8)),
        *per_a(lambda w: (64, w)),
        held(b, 256, B_WIDTH), held(b, 256, B_WIDTH), held(b, 256, B_WIDTH),
        held(b, 2, 32, B_WIDTH), held(b, 2, 64, B_WIDTH),
        held(b, 16, 16, 2 * B_QUARTER), held(b, 16, 16, 2 * B_QUARTER),
        held(b, 2, 64, B_WIDTH),
        dma((A_CHUNKS,)), dma((2, OTHERS)), dma((2, OTHERS)),
        dma((A_CHUNKS,)), dma((A_CHUNKS,)), dma((A_CHUNKS, 6)), dma((A_CHUNKS, 6)),
        dma((A_CHUNKS, OTHERS)), dma((A_CHUNKS, OTHERS)),
        dma((A_CHUNKS, OTHERS)), dma((A_CHUNKS, OTHERS)), dma((A_CHUNKS,)),
        dma((b,)), dma((b,)), dma((b, 6)), dma((b, 6)),
        dma((b, OTHERS)), dma((b, OTHERS)), dma((b,)),
    ]
    out = pl.pallas_call(
        kernel,
        out_shape=jax.ShapeDtypeStruct((3, 64, HIDDEN), BF),
        in_specs=[smem, smem, vmem, vmem, vmem, hbm],
        out_specs=hbm,
        scratch_shapes=scratch,
        compiler_params=pltpu.CompilerParams(
            collective_id=0, has_side_effects=True, vmem_limit_bytes=60 * 1024 * 1024
        ),
        name="rotate_and_place",
    )(placement, row_count, gate_proj, up_proj, down_proj, rotation)
    return jnp.transpose(out, (1, 0, 2))[None]


def solution(mesh):
    in_specs = (
        P(None, "hid", "ep"),
        P(None, "hid", "ep"),
        P(None, "ep", "hid"),
        P("hid", None),
        P(),
        P(),
    )
    out_specs = P("ep", "hid", None, None)
    return jax.shard_map(
        on_device, mesh=mesh, in_specs=in_specs, out_specs=out_specs, check_vma=False
    )
```

time: 255 us -> 87.9 us (0.34)
  waiting for transfers between devices: 188 us -> 0 us
  Pallas kernels: 0 us -> 84.2 us
  matrix products: 19 us -> 0 us
  blocking collectives: 16.6 us -> 0 us
  between operations: 14.1 us -> 0.01 us
  local copies, waits for them, and re-layouts: 11.8 us -> 3.49 us
  other arithmetic: 4.65 us -> 0 us
    all_gather x1 -> x0, waiting for transfers between devices: 120 us -> none  [on_device(): lax.all_gather(rotated[None], 'ep', axis=0, tiled=True)]
    pallas_call x0 -> x1, Pallas kernels: none -> 84.2 us  [on_device(): pl.pallas_call(kernel, out_shape=jax.ShapeDtypeStruct((3, 64, HIDDEN), BF...]
    reduce_scatter x1 -> x0, waiting for transfers between devices: 67.4 us -> none  [on_device(): lax.psum_scatter(jnp.einsum('fck,kh->fch', stacked, rotation, preferred_e...]
    dot_general x1 -> x0, matrix products: 19 us -> none  [on_device(): jnp.einsum('fck,kh->fch', stacked, rotation, preferred_element_type=jnp.f...]
    unnamed x1 -> x0, blocking collectives: 16.6 us -> none
    gather x2 -> x0, local copies, waits for them, and re-layouts: 8.17 us -> none  [assemble(): chosen = received[source_ids, :, expert_ids]]
  transfers between devices with their start and end apart: 2 -> 0, of which waited for: 2 -> 0; matrix products, arithmetic and copies ran while one was open for 1% -> 0% of each run, Pallas kernels for 0% -> 0%
where the time goes in v2:
time: 87.9 us; the launch traced here: 87.7 us
  Pallas kernels  84.2 us (96%)
  local copies, waits for them, and re-layouts  3.49 us (4%)
    pallas_call x1, Pallas kernels, on_device(): pl.pallas_call(kernel, out_shape=jax.ShapeDtypeStruct((3, 64, HIDDEN), BF...  84.2 us
    unnamed x1, local copies, waits for them, and re-layouts  3.49 us

profile of v2, /device:TPU:0, one launch (start us, length us, event | category | flops | bytes accessed | tf_op | source)
XLA Modules:
  0.0 87.7 jit_solution(2365245459201185298)
XLA Ops:
  0.0 84.2 %rotate_and_place.1 = bf16[3,64,7168]{2,1,0:T(8,128)(2,1)} custom-call(s32[2,16]{1,0:T(2,128)} %placement_ref.1, s32[2,16]{1,0:T(2,128)} %count_ref.1, bf16[2,896,128]{2,1,0:T(8,128)(2,1)} %gate_ref.1, bf16[2,896,128]{2,1,0:T(8,128)(2,1)} %up_ref.1, bf16[2,128,896]{2,1,0:T(8,128)(2,1)} %down_ref.1, bf16[896,7168]{1,0:T(8,128)(2,1)} %rot_hbm.1), custom_call_target="tpu_custom_call" | custom-call | tf_op jit(solution)/shard_map/rotate_and_place/pallas_call | solution.py:464
  84.2 3.5 %copy.8 = bf16[1,64,3,7168]{3,1,2,0:T(8,128)(2,1)} copy(bf16[1,64,3,7168]{3,1,2,0:T(8,128)(2,1)} %bitcast.3) | data formatting | bytes 5505024

commit v3 on v2

--- a/solution.py
+++ b/solution.py
@@ -104,7 +104,7 @@
 
 
 def kernel(
-    placement_ref, count_ref, gate_ref, up_ref, down_ref, rot_hbm, out_hbm, *scratch
+    placement_ref, count_ref, gate_ref, up_ref, down_ref, rot_hbm, *scratch
 ):
     scratch = list(scratch)
 
@@ -113,15 +113,18 @@
         del scratch[:count]
         return taken
 
-    rot, lhs_a, lhs_b, src, rcv, sel_a, put_a, sel_b, put_b, arrange = take(10)
-    a_core_out, a_core_in, a_own, a_far, a_from, a_sum, a_in, a_pick, a_got, a_out = (
-        take(A_CHUNKS) for _ in range(10)
+    a_got = take(A_CHUNKS)
+    b_got, put_hbm = take(2)
+    rot, lhs_a, lhs_b, src, rcv, sel_a, put_a, sel_b, arrange = take(9)
+    a_core_out, a_core_in, a_own, a_far, a_near, a_sum, a_in, a_pick = (
+        take(A_CHUNKS) for _ in range(8)
     )
-    b_core_out, b_core_in, b_own, b_far, b_from, b_pick, b_got, b_out = take(8)
-    rot_sem, src_send, src_recv = take(3)
-    a_core_send, a_core_recv, a_x_send, a_x_recv, a_in_send, a_in_recv = take(6)
-    a_own_send, a_own_recv, a_out_sem = take(3)
-    b_core_send, b_core_recv, b_x_send, b_x_recv, b_own_send, b_own_recv, b_out_sem = take(7)
+    b_core_out, b_core_in, b_own, b_far, b_near, b_pick = take(6)
+    rot_sem, put_sem, src_send, src_recv = take(4)
+    a_core_send, a_core_recv, a_x_send, a_far_recv, a_near_recv = take(5)
+    a_in_send, a_in_recv, a_own_send, a_own_recv, a_self = take(5)
+    b_core_send, b_core_recv, b_x_send, b_far_recv, b_near_recv = take(5)
+    b_own_send, b_own_recv, b_self = take(3)
 
     hid = lax.axis_index("hid")
     ep = lax.axis_index("ep")
@@ -137,6 +140,9 @@
             source, target, send, recv, device_id=(h, e), device_id_type=MESH
         )
 
+    def wait_bytes(ref, sem):
+        pltpu.make_async_copy(ref, ref, sem).wait()
+
     barrier = pltpu.get_barrier_semaphore()
     for h in (right, left, other):
         pl.semaphore_signal(barrier, 1, device_id=(h, ep), device_id_type=MESH)
@@ -149,26 +155,30 @@
 
     def src_copy(k, i):
         return remote(
-            src.at[k, peers[i]], rcv.at[k, ep], src_send.at[k, i], src_recv.at[k, i], hid, peers[i]
-        )
-
-    def x_copy(own, far, near, send, recv, half, i):
-        first, to, target = (
-            (0, right, far.at[0]),
-            (1, left, far.at[1]),
-            (3, right, near.at[0, pl.ds(half, half)]),
-            (4, left, near.at[1, pl.ds(0, half)]),
-            (2, right, near.at[0, pl.ds(0, half)]),
-            (5, left, near.at[1, pl.ds(half, half)]),
+            src.at[k, peers[i]], rcv.at[k, ep], src_send, src_recv, hid, peers[i]
+        )
+
+    def x_copy(own, far, near, send, far_recv, near_recv, half, i):
+        first, to, target, recv = (
+            (0, right, far.at[0], far_recv),
+            (1, left, far.at[1], far_recv),
+            (3, right, near.at[0, pl.ds(half, half)], near_recv),
+            (4, left, near.at[1, pl.ds(0, half)], near_recv),
+            (2, right, near.at[0, pl.ds(0, half)], near_recv),
+            (5, left, near.at[1, pl.ds(half, half)], near_recv),
         )[i]
-        return remote(own.at[pl.ds(first * half, half)], target, send.at[i], recv.at[i], to, ep)
+        return remote(own.at[pl.ds(first * half, half)], target, send, recv, to, ep)
 
     def a_x(c, i):
-        return x_copy(a_own[c], a_far[c], a_from[c], a_x_send.at[c], a_x_recv.at[c], 16, i)
+        return x_copy(
+            a_own[c], a_far[c], a_near[c],
+            a_x_send.at[c], a_far_recv.at[c], a_near_recv.at[c], 16, i,
+        )
 
     def b_x(n, i):
         return x_copy(
-            b_own.at[n], b_far.at[n], b_from.at[n], b_x_send.at[n], b_x_recv.at[n], 32, i
+            b_own.at[n], b_far.at[n], b_near.at[n],
+            b_x_send, b_far_recv.at[n], b_near_recv.at[n], 32, i,
         )
 
     def a_core(c):
@@ -176,36 +186,32 @@
 
     def b_core(n):
         return remote(
-            b_core_out.at[n], b_core_in.at[n], b_core_send.at[n], b_core_recv.at[n], other, ep
+            b_core_out.at[n], b_core_in.at[n], b_core_send, b_core_recv.at[n], other, ep
         )
 
     def a_spread(c, i):
         return remote(
-            a_sum[c].at[peers[i]], a_in[c].at[ep], a_in_send.at[c, i], a_in_recv.at[c, i],
-            hid, peers[i],
+            a_sum[c].at[peers[i]], a_in[c].at[ep], a_in_send.at[c], a_in_recv.at[c], hid, peers[i]
         )
 
     def a_owner(c, i):
         return remote(
-            a_pick[c].at[peers[i]], a_got[c].at[ep], a_own_send.at[c, i], a_own_recv.at[c, i],
+            a_pick[c].at[peers[i]], a_got[c].at[ep], a_own_send.at[c], a_own_recv.at[c],
             hid, peers[i],
         )
+
+    def a_keep(c):
+        return pltpu.make_async_copy(a_pick[c].at[ep], a_got[c].at[ep], a_self.at[c])
 
     def b_owner(n, i):
         return remote(
-            b_pick.at[n, peers[i]], b_got.at[n, ep], b_own_send.at[n, i], b_own_recv.at[n, i],
-            hid, peers[i],
-        )
-
-    def a_store(c):
-        columns = pl.ds(A_STARTS[c], A_WIDTHS[c])
-        return pltpu.make_async_copy(a_out[c], out_hbm.at[0, :, columns], a_out_sem.at[c])
-
-    def b_store(n):
-        columns = pl.ds(pl.multiple_of(n * B_WIDTH, B_WIDTH), B_WIDTH)
-        return pltpu.make_async_copy(
-            b_out.at[n], out_hbm.at[pl.ds(1, 2), :, columns], b_out_sem.at[n]
-        )
+            b_pick.at[n, peers[i]], b_got.at[n, ep], b_own_send, b_own_recv, hid, peers[i]
+        )
+
+    def b_keep(n):
+        return pltpu.make_async_copy(b_pick.at[n, ep], b_got.at[n, ep], b_self)
+
+    put_copy = pltpu.make_async_copy(put_a, put_hbm, put_sem)
 
     def sum_cores(own, core_in, half, start_x):
         own[0:2 * half] += core_in[0:2 * half]
@@ -216,11 +222,10 @@
         start_x(3)
         own[6 * half:8 * half] += core_in[6 * half:8 * half]
 
-    def pass_on(own, far, half, x_of):
-        x_of(0).wait_recv()
+    def pass_on(own, far, far_recv, half, x_of):
+        wait_bytes(far, far_recv)
         own[2 * half:3 * half] += far[0]
         x_of(4).start()
-        x_of(1).wait_recv()
         own[5 * half:6 * half] += far[1]
         x_of(5).start()
 
@@ -247,16 +252,15 @@
         sum_cores(a_own[c], a_core_in[c], 16, lambda i: a_x(c, i).start())
 
     def a_pass_on(c):
-        pass_on(a_own[c], a_far[c], 16, lambda i: a_x(c, i))
+        pass_on(a_own[c], a_far[c], a_far_recv.at[c], 16, lambda i: a_x(c, i))
 
     def a_to_peers(c):
-        for i in range(2, 6):
-            a_x(c, i).wait_recv()
+        wait_bytes(a_near[c], a_near_recv.at[c])
         eighth = A_WIDTHS[c] // 8
         for m in range(2):
             for q in range(8):
                 a_sum[c][m * 8 + q] = total_of(
-                    a_own[c], a_from[c], 16,
+                    a_own[c], a_near[c], 16,
                     slice(m * 16, m * 16 + 16), slice(q * eighth, (q + 1) * eighth),
                 )
         for i in range(OTHERS):
@@ -264,23 +268,13 @@
         a_in[c][ep] = a_sum[c][ep]
 
     def a_to_owners(c):
-        for i in range(OTHERS):
-            a_spread(c, i).wait_recv()
+        wait_bytes(a_in[c].at[pl.ds(0, OTHERS)], a_in_recv.at[c])
         eighth = A_WIDTHS[c] // 8
         rows = dot(sel_a[...], a_in[c][...].reshape(256, eighth))
         a_pick[c][...] = rows.astype(BF).reshape(16, 32, eighth)
         for i in range(OTHERS):
             a_owner(c, i).start()
-        a_got[c][ep] = a_pick[c][ep]
-
-    def a_place(c):
-        for i in range(OTHERS):
-            a_owner(c, i).wait_recv()
-        eighth = A_WIDTHS[c] // 8
-        for q in range(8):
-            both = jnp.concatenate([a_got[c][q], a_got[c][8 + q]], axis=0)
-            a_out[c][:, q * eighth:(q + 1) * eighth] = dot(put_a[...], both).astype(BF)
-        a_store(c).start()
+        a_keep(c).start()
 
     def b_multiply(n):
         here = pl.ds(pl.multiple_of(n * B_WIDTH, B_WIDTH), B_WIDTH)
@@ -294,34 +288,22 @@
         sum_cores(b_own.at[n], b_core_in.at[n], 32, lambda i: b_x(n, i).start())
 
     def b_pass_on(n):
-        pass_on(b_own.at[n], b_far.at[n], 32, lambda i: b_x(n, i))
+        pass_on(b_own.at[n], b_far.at[n], b_far_recv.at[n], 32, lambda i: b_x(n, i))
 
     def b_to_owners(n):
-        for i in range(2, 6):
-            b_x(n, i).wait_recv()
+        wait_bytes(b_near.at[n], b_near_recv.at[n])
         quarters = []
         for g in range(4):
             columns = slice(g * B_QUARTER, (g + 1) * B_QUARTER)
             quarters.append(jnp.concatenate([
-                total_of(b_own.at[n], b_from.at[n], 32, slice(k * 32, k * 32 + 32), columns)
+                total_of(b_own.at[n], b_near.at[n], 32, slice(k * 32, k * 32 + 32), columns)
                 for k in range(2)
             ], axis=1))
         rows = dot(sel_b[...], jnp.concatenate(quarters, axis=0))
         b_pick[n] = rows.astype(BF).reshape(16, 16, 2 * B_QUARTER)
         for i in range(OTHERS):
             b_owner(n, i).start()
-        b_got[n, ep] = b_pick[n, ep]
-
-    def b_place(n):
-        for i in range(OTHERS):
-            b_owner(n, i).wait_recv()
-        rows = dot(put_b[...], b_got[n].reshape(256, 2 * B_QUARTER)).astype(BF)
-        for k in range(2):
-            for g in range(4):
-                b_out[n, k, :, g * B_QUARTER:(g + 1) * B_QUARTER] = rows[
-                    g * 64:(g + 1) * 64, k * B_QUARTER:(k + 1) * B_QUARTER
-                ]
-        b_store(n).start()
+        b_keep(n).start()
 
     for c in range(A_CHUNKS):
         rot_copy(c).start()
@@ -349,9 +331,8 @@
     low, high, mine = ranges(hid, ep, placement_ref, count_ref)
     sel_a[...] = select_a(ep, low, high)
     put_a[...] = place_a(mine)
+    put_copy.start()
     sel_b[...] = select_b(low, high)
-    r, s = iotas(256, 256)
-    put_b[...] = onehot(s == (r % 16) * 16 + ((r // 16) % 4) * 4 + r // 64)
     r, s = iotas(512, 512)
     block = ((x + ring_offset((r // 64) % 4)) % 4) * 2 + jnp.where(r < 256, 1 - core, core)
     arrange[...] = onehot(
@@ -374,22 +355,19 @@
     a_to_peers(0)
     a_pass_on(2)
 
-    for k in range(2):
-        for i in range(OTHERS):
-            src_copy(k, i).wait_recv()
+    wait_bytes(rcv.at[:, pl.ds(0, OTHERS)], src_recv)
     lhs_b[...] = dot(arrange[...], rcv[...].reshape(512, PIECE)).astype(BF)
     b_multiply(0)
     a_to_peers(1)
 
-    stages = ((b_sum_cores, 0), (b_multiply, -1), (b_pass_on, 1), (b_to_owners, 2), (b_place, 3))
+    stages = ((b_sum_cores, 0), (b_multiply, -1), (b_pass_on, 1), (b_to_owners, 2))
     extras = {
         0: (lambda: a_to_owners(0), lambda: a_to_peers(2)),
         1: (lambda: a_to_owners(1),),
-        2: (lambda: a_to_owners(2), lambda: a_place(0), lambda: a_place(1)),
-        3: (lambda: a_place(2),),
+        2: (lambda: a_to_owners(2),),
     }
 
-    @pl.loop(0, B_CHUNKS + 3)
+    @pl.loop(0, B_CHUNKS + 2)
     def _(t):
         for stage, lag in stages:
             @pl.when((t >= lag) & (t < B_CHUNKS + lag))
@@ -401,25 +379,74 @@
                 for one in work:
                     one()
 
-    for k in range(2):
-        for i in range(OTHERS):
-            src_copy(k, i).wait_send()
+    rest = pl.ds(0, OTHERS)
+    put_copy.wait()
+    wait_bytes(src.at[:, rest], src_send)
     for c in range(A_CHUNKS):
         a_core(c).wait_send()
-        for i in range(6):
-            a_x(c, i).wait_send()
-        for i in range(OTHERS):
-            a_spread(c, i).wait_send()
-            a_owner(c, i).wait_send()
+        wait_bytes(a_own[c].at[pl.ds(0, 96)], a_x_send.at[c])
+        wait_bytes(a_sum[c].at[rest], a_in_send.at[c])
+        wait_bytes(a_pick[c].at[rest], a_own_send.at[c])
+        a_keep(c).wait()
+        wait_bytes(a_got[c].at[rest], a_own_recv.at[c])
+    wait_bytes(b_core_out, b_core_send)
+    wait_bytes(b_own.at[:, pl.ds(0, 192)], b_x_send)
+    wait_bytes(b_pick.at[:, rest], b_own_send)
+    wait_bytes(b_pick.at[:, 0], b_self)
+    wait_bytes(b_got.at[:, rest], b_own_recv)
+
+
+def place_kernel(*refs):
+    a_got, (b_got, put_hbm, out_hbm) = refs[:A_CHUNKS], refs[A_CHUNKS:A_CHUNKS + 3]
+    a_in, (b_in, put_a) = refs[A_CHUNKS + 3:2 * A_CHUNKS + 3], refs[2 * A_CHUNKS + 3:2 * A_CHUNKS + 5]
+    a_out, b_out, a_load, b_load, put_load, a_sem, b_sem = refs[2 * A_CHUNKS + 5:]
+
+    def a_read(c):
+        return pltpu.make_async_copy(a_got[c], a_in[c], a_load.at[c])
+
+    def b_read(n):
+        return pltpu.make_async_copy(b_got.at[n], b_in.at[n], b_load.at[n])
+
+    def a_store(c):
+        columns = pl.ds(A_STARTS[c], A_WIDTHS[c])
+        return pltpu.make_async_copy(a_out.at[:, columns], out_hbm.at[0, :, columns], a_sem.at[c])
+
+    def b_store(n):
+        columns = pl.ds(pl.multiple_of(n * B_WIDTH, B_WIDTH), B_WIDTH)
+        return pltpu.make_async_copy(
+            b_out.at[:, :, columns], out_hbm.at[pl.ds(1, 2), :, columns], b_sem.at[n]
+        )
+
+    put_copy = pltpu.make_async_copy(put_hbm, put_a, put_load)
+    put_copy.start()
+    for c in range(A_CHUNKS):
+        a_read(c).start()
+    for n in range(B_CHUNKS):
+        b_read(n).start()
+    r, s = iotas(256, 256)
+    put_b = onehot(s == (r % 16) * 16 + ((r // 16) % 4) * 4 + r // 64)
+    put_copy.wait()
+    for c in range(A_CHUNKS):
+        a_read(c).wait()
+        eighth = A_WIDTHS[c] // 8
+        for q in range(8):
+            both = jnp.concatenate([a_in[c][q], a_in[c][8 + q]], axis=0)
+            first = A_STARTS[c] + q * eighth
+            a_out[:, first:first + eighth] = dot(put_a[...], both).astype(BF)
+        a_store(c).start()
+    for n in range(B_CHUNKS):
+        b_read(n).wait()
+        rows = dot(put_b, b_in[n].reshape(256, 2 * B_QUARTER)).astype(BF)
+        for k in range(2):
+            for g in range(4):
+                first = n * B_WIDTH + g * B_QUARTER
+                b_out[k, :, first:first + B_QUARTER] = rows[
+                    g * 64:(g + 1) * 64, k * B_QUARTER:(k + 1) * B_QUARTER
+                ]
+        b_store(n).start()
+    for c in range(A_CHUNKS):
         a_store(c).wait()
-
-    @pl.loop(0, B_CHUNKS)
-    def _(n):
-        b_core(n).wait_send()
-        for i in range(6):
-            b_x(n, i).wait_send()
-        for i in range(OTHERS):
-            b_owner(n, i).wait_send()
+    for n in range(B_CHUNKS):
         b_store(n).wait()
 
 
@@ -439,7 +466,7 @@
     scratch = [
         held(PIECE, HIDDEN), held(256, PIECE), held(512, PIECE),
         held(2, 16, 16, PIECE), held(2, 16, 16, PIECE),
-        held(512, 256), held(64, 64), held(256, 128), held(256, 256), held(512, 512),
+        held(512, 256), held(64, 64), held(256, 128), held(512, 512),
         *per_a(lambda w: (128, w)),
         *per_a(lambda w: (128, w)),
         *per_a(lambda w: (128, w)),
@@ -448,30 +475,45 @@
         *per_a(lambda w: (16, 16, w // 8)),
         *per_a(lambda w: (16, 16, w // 8)),
         *per_a(lambda w: (16, 32, w // 8)),
-        *per_a(lambda w: (16, 32, w // 8)),
-        *per_a(lambda w: (64, w)),
         held(b, 256, B_WIDTH), held(b, 256, B_WIDTH), held(b, 256, B_WIDTH),
         held(b, 2, 32, B_WIDTH), held(b, 2, 64, B_WIDTH),
-        held(b, 16, 16, 2 * B_QUARTER), held(b, 16, 16, 2 * B_QUARTER),
-        held(b, 2, 64, B_WIDTH),
-        dma((A_CHUNKS,)), dma((2, OTHERS)), dma((2, OTHERS)),
-        dma((A_CHUNKS,)), dma((A_CHUNKS,)), dma((A_CHUNKS, 6)), dma((A_CHUNKS, 6)),
-        dma((A_CHUNKS, OTHERS)), dma((A_CHUNKS, OTHERS)),
-        dma((A_CHUNKS, OTHERS)), dma((A_CHUNKS, OTHERS)), dma((A_CHUNKS,)),
-        dma((b,)), dma((b,)), dma((b, 6)), dma((b, 6)),
-        dma((b, OTHERS)), dma((b, OTHERS)), dma((b,)),
+        held(b, 16, 16, 2 * B_QUARTER),
+        dma((A_CHUNKS,)), dma, dma, dma,
+        dma((A_CHUNKS,)), dma((A_CHUNKS,)), dma((A_CHUNKS,)), dma((A_CHUNKS,)), dma((A_CHUNKS,)),
+        dma((A_CHUNKS,)), dma((A_CHUNKS,)), dma((A_CHUNKS,)), dma((A_CHUNKS,)), dma((A_CHUNKS,)),
+        dma, dma((b,)), dma, dma((b,)), dma((b,)),
+        dma, dma, dma,
     ]
-    out = pl.pallas_call(
+    arrived = [
+        *(jax.ShapeDtypeStruct((16, 32, w // 8), BF) for w in A_WIDTHS),
+        jax.ShapeDtypeStruct((b, 16, 16, 2 * B_QUARTER), BF),
+        jax.ShapeDtypeStruct((64, 64), BF),
+    ]
+    limit = 60 * 1024 * 1024
+    got = pl.pallas_call(
         kernel,
-        out_shape=jax.ShapeDtypeStruct((3, 64, HIDDEN), BF),
+        out_shape=arrived,
         in_specs=[smem, smem, vmem, vmem, vmem, hbm],
-        out_specs=hbm,
+        out_specs=[hbm] * len(arrived),
         scratch_shapes=scratch,
         compiler_params=pltpu.CompilerParams(
-            collective_id=0, has_side_effects=True, vmem_limit_bytes=60 * 1024 * 1024
+            collective_id=0, has_side_effects=True, vmem_limit_bytes=limit
         ),
-        name="rotate_and_place",
+        name="rotate_and_send",
     )(placement, row_count, gate_proj, up_proj, down_proj, rotation)
+    out = pl.pallas_call(
+        place_kernel,
+        out_shape=jax.ShapeDtypeStruct((3, 64, HIDDEN), BF),
+        in_specs=[hbm] * len(got),
+        out_specs=hbm,
+        scratch_shapes=[
+            *(held(*v.shape) for v in arrived),
+            held(64, HIDDEN), held(2, 64, HIDDEN),
+            dma((A_CHUNKS,)), dma((b,)), dma, dma((A_CHUNKS,)), dma((b,)),
+        ],
+        compiler_params=pltpu.CompilerParams(vmem_limit_bytes=limit),
+        name="place",
+    )(*got)
     return jnp.transpose(out, (1, 0, 2))[None]
 
 

time: 87.9 us -> 75.8 us (0.86)
  Pallas kernels: 84.2 us -> 75.6 us
  local copies, waits for them, and re-layouts: 3.49 us -> 0 us
    pallas_call x1 -> x2, Pallas kernels: 84.2 us -> 75.6 us  [the longest x1 71.1 us: on_device(): pl.pallas_call(kernel, out_shape=arrived, in_specs=[smem, smem, vmem, vme...]
    unnamed x1 -> x0, local copies, waits for them, and re-layouts: 3.49 us -> none
where the time goes in v3:
time: 75.8 us; the launch traced here: 75.6 us
  Pallas kernels  75.6 us (100%)
    pallas_call x1, Pallas kernels, on_device(): pl.pallas_call(kernel, out_shape=arrived, in_specs=[smem, smem, vmem, vme...  71.1 us
    pallas_call x1, Pallas kernels, on_device(): pl.pallas_call(place_kernel, out_shape=jax.ShapeDtypeStruct((3, 64, HIDDE...  4.49 us

profile of v3, /device:TPU:0, one launch (start us, length us, event | category | flops | bytes accessed | tf_op | source)
XLA Modules:
  0.0 75.6 jit_solution(5131727449936768005)
XLA Ops:
  0.0 71.1 %rotate_and_send.1 = (bf16[16,32,128]{2,1,0:T(8,128)(2,1)}, bf16[16,32,256]{2,1,0:T(8,128)(2,1)}, bf16[16,32,512]{2,1,0:T(8,128)(2,1)}, bf16[7,16,16,512]{3,2,1,0:T(8,128)(2,1)}, bf16[64,64]{1,0:T(8,128)(2,1)}) custom-call(s32[2,16]{1,0:T(2,128)} %placement_ref.1, s32[2,16]{1,0:T(2,128)} %count_ref.1, bf16[2,896,128]{2,1,0:T(8,128)(2,1)} %gate_ref.1, ...), custom_call_target="tpu_custom_call" | custom-call | tf_op jit(solution)/shard_map/rotate_and_send/pallas_call | solution.py:493
  71.1 4.5 %place.1 = bf16[3,64,7168]{2,1,0:T(8,128)(2,1)} custom-call(bf16[16,32,128]{2,1,0:T(8,128)(2,1)} %get-tuple-element.10.refs_0_, bf16[16,32,256]{2,1,0:T(8,128)(2,1)} %get-tuple-element.11.refs_1_, bf16[16,32,512]{2,1,0:T(8,128)(2,1)} %get-tuple-element.12.refs_2_, bf16[7,16,16,512]{3,2,1,0:T(8,128)(2,1)} %get-tuple-element.13.refs_3_, ...), custom_call_target="tpu_custom_call" | custom-call | tf_op jit(solution)/shard_map/place/pallas_call | solution.py:504

commit v4 on v3

--- a/solution.py
+++ b/solution.py
@@ -15,12 +15,14 @@
 OTHERS = len(PEERS)
 HIDDEN = 7168
 PIECE = 896
-A_WIDTHS = (1024, 2048, 4096)
-A_STARTS = (0, 1024, 3072)
+A_WIDTHS = (1024, 2048, 2048, 2048)
+A_STARTS = (0, 1024, 3072, 5120)
 A_CHUNKS = len(A_WIDTHS)
 B_WIDTH = 1024
-B_CHUNKS = HIDDEN // B_WIDTH
-B_QUARTER = B_WIDTH // 4
+B_CHUNKS = 6
+C_WIDTH = 512
+C_START = B_CHUNKS * B_WIDTH
+C_CHUNKS = (HIDDEN - C_START) // C_WIDTH
 TILE = 1024
 
 
@@ -104,7 +106,7 @@
 
 
 def kernel(
-    placement_ref, count_ref, gate_ref, up_ref, down_ref, rot_hbm, *scratch
+    placement_ref, count_ref, gate_hbm, up_hbm, down_hbm, rot_hbm, *scratch
 ):
     scratch = list(scratch)
 
@@ -114,17 +116,22 @@
         return taken
 
     a_got = take(A_CHUNKS)
-    b_got, put_hbm = take(2)
+    b_got, *c_got = take(1 + C_CHUNKS)
+    (put_hbm,) = take(1)
+    gate, up, down = take(3)
     rot, lhs_a, lhs_b, src, rcv, sel_a, put_a, sel_b, arrange = take(9)
     a_core_out, a_core_in, a_own, a_far, a_near, a_sum, a_in, a_pick = (
         take(A_CHUNKS) for _ in range(8)
     )
     b_core_out, b_core_in, b_own, b_far, b_near, b_pick = take(6)
-    rot_sem, put_sem, src_send, src_recv = take(4)
+    c_core_out, c_core_in, c_own, c_far, c_near, c_pick = (take(C_CHUNKS) for _ in range(6))
+    in_sem, rot_sem, put_sem, src_send, src_recv = take(5)
     a_core_send, a_core_recv, a_x_send, a_far_recv, a_near_recv = take(5)
     a_in_send, a_in_recv, a_own_send, a_own_recv, a_self = take(5)
     b_core_send, b_core_recv, b_x_send, b_far_recv, b_near_recv = take(5)
     b_own_send, b_own_recv, b_self = take(3)
+    c_core_send, c_core_recv, c_x_send, c_far_recv, c_near_recv = take(5)
+    c_own_send, c_own_recv, c_self = take(3)
 
     hid = lax.axis_index("hid")
     ep = lax.axis_index("ep")
@@ -153,9 +160,9 @@
         columns = pl.ds(A_STARTS[c], A_WIDTHS[c])
         return pltpu.make_async_copy(rot_hbm.at[:, columns], rot.at[:, columns], rot_sem.at[c])
 
-    def src_copy(k, i):
+    def src_copy(i):
         return remote(
-            src.at[k, peers[i]], rcv.at[k, ep], src_send, src_recv, hid, peers[i]
+            src.at[peers[i]], rcv.at[ep], src_send, src_recv, hid, peers[i]
         )
 
     def x_copy(own, far, near, send, far_recv, near_recv, half, i):
@@ -181,6 +188,24 @@
             b_x_send, b_far_recv.at[n], b_near_recv.at[n], 32, i,
         )
 
+    def c_x(n, i):
+        return x_copy(
+            c_own[n], c_far[n], c_near[n],
+            c_x_send.at[n], c_far_recv.at[n], c_near_recv.at[n], 32, i,
+        )
+
+    def c_core(n):
+        return remote(c_core_out[n], c_core_in[n], c_core_send.at[n], c_core_recv.at[n], other, ep)
+
+    def c_owner(n, i):
+        return remote(
+            c_pick[n].at[peers[i]], c_got[n].at[ep], c_own_send.at[n], c_own_recv.at[n],
+            hid, peers[i],
+        )
+
+    def c_keep(n):
+        return pltpu.make_async_copy(c_pick[n].at[ep], c_got[n].at[ep], c_self.at[n])
+
     def a_core(c):
         return remote(a_core_out[c], a_core_in[c], a_core_send.at[c], a_core_recv.at[c], other, ep)
 
@@ -212,6 +237,10 @@
         return pltpu.make_async_copy(b_pick.at[n, ep], b_got.at[n, ep], b_self)
 
     put_copy = pltpu.make_async_copy(put_a, put_hbm, put_sem)
+    in_copies = [
+        pltpu.make_async_copy(source, target, in_sem.at[i])
+        for i, (source, target) in enumerate(((gate_hbm, gate), (up_hbm, up), (down_hbm, down)))
+    ]
 
     def sum_cores(own, core_in, half, start_x):
         own[0:2 * half] += core_in[0:2 * half]
@@ -276,11 +305,25 @@
             a_owner(c, i).start()
         a_keep(c).start()
 
+    def multiply(width, start, core_out, own):
+        total = dot(lhs_b[...], rot[:, pl.ds(start, width)])
+        core_out[...] = total[:256].astype(BF)
+        own[...] = total[256:].astype(BF)
+
+    def pick_rows(width, own, near, pick):
+        quarter = width // 4
+        quarters = []
+        for g in range(4):
+            columns = slice(g * quarter, (g + 1) * quarter)
+            quarters.append(jnp.concatenate([
+                total_of(own, near, 32, slice(k * 32, k * 32 + 32), columns) for k in range(2)
+            ], axis=1))
+        rows = dot(sel_b[...], jnp.concatenate(quarters, axis=0))
+        pick[...] = rows.astype(BF).reshape(16, 16, 2 * quarter)
+
     def b_multiply(n):
-        here = pl.ds(pl.multiple_of(n * B_WIDTH, B_WIDTH), B_WIDTH)
-        total = dot(lhs_b[...], rot[:, here])
-        b_core_out[n] = total[:256].astype(BF)
-        b_own[n] = total[256:].astype(BF)
+        start = pl.multiple_of(n * B_WIDTH, B_WIDTH)
+        multiply(B_WIDTH, start, b_core_out.at[n], b_own.at[n])
         b_core(n).start()
 
     def b_sum_cores(n):
@@ -292,19 +335,31 @@
 
     def b_to_owners(n):
         wait_bytes(b_near.at[n], b_near_recv.at[n])
-        quarters = []
-        for g in range(4):
-            columns = slice(g * B_QUARTER, (g + 1) * B_QUARTER)
-            quarters.append(jnp.concatenate([
-                total_of(b_own.at[n], b_near.at[n], 32, slice(k * 32, k * 32 + 32), columns)
-                for k in range(2)
-            ], axis=1))
-        rows = dot(sel_b[...], jnp.concatenate(quarters, axis=0))
-        b_pick[n] = rows.astype(BF).reshape(16, 16, 2 * B_QUARTER)
+        pick_rows(B_WIDTH, b_own.at[n], b_near.at[n], b_pick.at[n])
         for i in range(OTHERS):
             b_owner(n, i).start()
         b_keep(n).start()
 
+    def c_multiply(n):
+        multiply(C_WIDTH, C_START + n * C_WIDTH, c_core_out[n], c_own[n])
+        c_core(n).start()
+
+    def c_sum_cores(n):
+        c_core(n).wait_recv()
+        sum_cores(c_own[n], c_core_in[n], 32, lambda i: c_x(n, i).start())
+
+    def c_pass_on(n):
+        pass_on(c_own[n], c_far[n], c_far_recv.at[n], 32, lambda i: c_x(n, i))
+
+    def c_to_owners(n):
+        wait_bytes(c_near[n], c_near_recv.at[n])
+        pick_rows(C_WIDTH, c_own[n], c_near[n], c_pick[n])
+        for i in range(OTHERS):
+            c_owner(n, i).start()
+        c_keep(n).start()
+
+    for copy in in_copies:
+        copy.start()
     for c in range(A_CHUNKS):
         rot_copy(c).start()
 
@@ -312,62 +367,69 @@
     block = ((x + ring_offset((r // 32) % 4)) % 4) * 2 + jnp.where(r < 128, 1 - core, core)
     column = block * 16 + r % 16
     expert = (r // 16) % 2
-    rows = sum(dot_t(onehot((expert == m) & (s == column)), gate_ref[m]) for m in range(2))
+    in_copies[0].wait()
+    rows = sum(dot_t(onehot((expert == m) & (s == column)), gate[m]) for m in range(2))
     lhs_a[...] = rows.astype(BF)
 
     column = (r % 8) * 16 + r // 16
     expert = (r // 8) % 2
     spread = [onehot((expert == m) & (s == column)) for m in range(2)]
-    rows = sum(dot_t(spread[m], up_ref[m]) for m in range(2))
-    src[0] = rows.astype(BF).reshape(16, 16, PIECE)
-    rows = sum(dot(spread[m], down_ref[m]) for m in range(2))
-    src[1] = rows.astype(BF).reshape(16, 16, PIECE)
-    for k in range(2):
-        rcv[k, ep] = src[k, ep]
-
-    for c in range(A_CHUNKS):
-        a_multiply(c)
-
+    in_copies[1].wait()
+    rows = sum(dot_t(spread[m], up[m]) for m in range(2))
+    src[:, 0] = rows.astype(BF).reshape(16, 16, PIECE)
+    in_copies[2].wait()
+    rows = sum(dot(spread[m], down[m]) for m in range(2))
+    src[:, 1] = rows.astype(BF).reshape(16, 16, PIECE)
+    a_multiply(0)
+
+    pl.semaphore_wait(barrier, 3 + OTHERS)
+
+    a_core(0).start()
+    for i in range(OTHERS):
+        src_copy(i).start()
+    a_multiply(1)
+    a_core(1).start()
+    a_sum_cores(0)
+    a_multiply(2)
+    a_core(2).start()
+    a_sum_cores(1)
+    a_pass_on(0)
+    a_multiply(3)
+    a_core(3).start()
+    a_sum_cores(2)
+    a_pass_on(1)
+    rcv[ep] = src[ep]
     low, high, mine = ranges(hid, ep, placement_ref, count_ref)
     sel_a[...] = select_a(ep, low, high)
+    a_to_peers(0)
+    a_sum_cores(3)
+    a_pass_on(2)
+    r, s = iotas(512, 512)
+    block = ((x + ring_offset((r // 64) % 4)) % 4) * 2 + jnp.where(r < 256, 1 - core, core)
+    arrange[...] = onehot(
+        s == (r % 16) * 32 + ((r // 32) % 2) * 16 + ((r // 16) % 2) * 8 + block
+    )
     put_a[...] = place_a(mine)
     put_copy.start()
     sel_b[...] = select_b(low, high)
-    r, s = iotas(512, 512)
-    block = ((x + ring_offset((r // 64) % 4)) % 4) * 2 + jnp.where(r < 256, 1 - core, core)
-    arrange[...] = onehot(
-        s == ((r // 32) % 2) * 256 + (r % 16) * 16 + ((r // 16) % 2) * 8 + block
-    )
-
-    pl.semaphore_wait(barrier, 3 + OTHERS)
-
-    for c in range(A_CHUNKS):
-        a_core(c).start()
-    for i in range(OTHERS):
-        src_copy(0, i).start()
-    a_sum_cores(0)
-    for i in range(OTHERS):
-        src_copy(1, i).start()
-    a_sum_cores(1)
-    a_pass_on(0)
-    a_sum_cores(2)
-    a_pass_on(1)
-    a_to_peers(0)
-    a_pass_on(2)
-
-    wait_bytes(rcv.at[:, pl.ds(0, OTHERS)], src_recv)
+    a_to_peers(1)
+    a_pass_on(3)
+
+    wait_bytes(rcv.at[pl.ds(0, OTHERS)], src_recv)
     lhs_b[...] = dot(arrange[...], rcv[...].reshape(512, PIECE)).astype(BF)
     b_multiply(0)
-    a_to_peers(1)
+    a_to_owners(0)
+    a_to_peers(2)
 
     stages = ((b_sum_cores, 0), (b_multiply, -1), (b_pass_on, 1), (b_to_owners, 2))
     extras = {
-        0: (lambda: a_to_owners(0), lambda: a_to_peers(2)),
-        1: (lambda: a_to_owners(1),),
-        2: (lambda: a_to_owners(2),),
+        0: (lambda: a_to_owners(1), lambda: a_to_peers(3)),
+        1: (lambda: a_to_owners(2),),
+        2: (lambda: a_to_owners(3),),
+        B_CHUNKS - 1: (lambda: c_multiply(0),),
     }
 
-    @pl.loop(0, B_CHUNKS + 2)
+    @pl.loop(0, B_CHUNKS)
     def _(t):
         for stage, lag in stages:
             @pl.when((t >= lag) & (t < B_CHUNKS + lag))
@@ -379,9 +441,20 @@
                 for one in work:
                     one()
 
+    c_sum_cores(0)
+    c_multiply(1)
+    b_pass_on(B_CHUNKS - 1)
+    b_to_owners(B_CHUNKS - 2)
+    c_sum_cores(1)
+    c_pass_on(0)
+    b_to_owners(B_CHUNKS - 1)
+    c_pass_on(1)
+    c_to_owners(0)
+    c_to_owners(1)
+
     rest = pl.ds(0, OTHERS)
     put_copy.wait()
-    wait_bytes(src.at[:, rest], src_send)
+    wait_bytes(src.at[rest], src_send)
     for c in range(A_CHUNKS):
         a_core(c).wait_send()
         wait_bytes(a_own[c].at[pl.ds(0, 96)], a_x_send.at[c])
@@ -394,65 +467,77 @@
     wait_bytes(b_pick.at[:, rest], b_own_send)
     wait_bytes(b_pick.at[:, 0], b_self)
     wait_bytes(b_got.at[:, rest], b_own_recv)
+    for n in range(C_CHUNKS):
+        c_core(n).wait_send()
+        wait_bytes(c_own[n].at[pl.ds(0, 192)], c_x_send.at[n])
+        wait_bytes(c_pick[n].at[rest], c_own_send.at[n])
+        c_keep(n).wait()
+        wait_bytes(c_got[n].at[rest], c_own_recv.at[n])
 
 
 def place_kernel(*refs):
-    a_got, (b_got, put_hbm, out_hbm) = refs[:A_CHUNKS], refs[A_CHUNKS:A_CHUNKS + 3]
-    a_in, (b_in, put_a) = refs[A_CHUNKS + 3:2 * A_CHUNKS + 3], refs[2 * A_CHUNKS + 3:2 * A_CHUNKS + 5]
-    a_out, b_out, a_load, b_load, put_load, a_sem, b_sem = refs[2 * A_CHUNKS + 5:]
-
-    def a_read(c):
-        return pltpu.make_async_copy(a_got[c], a_in[c], a_load.at[c])
-
-    def b_read(n):
-        return pltpu.make_async_copy(b_got.at[n], b_in.at[n], b_load.at[n])
-
-    def a_store(c):
-        columns = pl.ds(A_STARTS[c], A_WIDTHS[c])
-        return pltpu.make_async_copy(a_out.at[:, columns], out_hbm.at[0, :, columns], a_sem.at[c])
-
-    def b_store(n):
-        columns = pl.ds(pl.multiple_of(n * B_WIDTH, B_WIDTH), B_WIDTH)
-        return pltpu.make_async_copy(
-            b_out.at[:, :, columns], out_hbm.at[pl.ds(1, 2), :, columns], b_sem.at[n]
-        )
-
+    refs = list(refs)
+
+    def take(count):
+        taken = refs[:count]
+        del refs[:count]
+        return taken
+
+    a_got, (b_got,), c_got, (put_hbm, out_hbm) = take(A_CHUNKS), take(1), take(C_CHUNKS), take(2)
+    a_in, (b_in,), c_in, (put_a,) = take(A_CHUNKS), take(1), take(C_CHUNKS), take(1)
+    a_out, b_out, put_load, a_load, b_load, c_load, a_sem, b_sem, c_sem = refs
+
+    chunks = [
+        (b_got.at[n], b_in.at[n], b_load.at[n], b_sem.at[n], n * B_WIDTH, B_WIDTH)
+        for n in range(B_CHUNKS)
+    ] + [
+        (c_got[n], c_in[n], c_load.at[n], c_sem.at[n], C_START + n * C_WIDTH, C_WIDTH)
+        for n in range(C_CHUNKS)
+    ]
     put_copy = pltpu.make_async_copy(put_hbm, put_a, put_load)
+    a_reads = [pltpu.make_async_copy(a_got[c], a_in[c], a_load.at[c]) for c in range(A_CHUNKS)]
+    reads = [pltpu.make_async_copy(got, held, load) for got, held, load, *_ in chunks]
+    stores = []
     put_copy.start()
-    for c in range(A_CHUNKS):
-        a_read(c).start()
-    for n in range(B_CHUNKS):
-        b_read(n).start()
+    for copy in a_reads + reads:
+        copy.start()
     r, s = iotas(256, 256)
     put_b = onehot(s == (r % 16) * 16 + ((r // 16) % 4) * 4 + r // 64)
     put_copy.wait()
     for c in range(A_CHUNKS):
-        a_read(c).wait()
-        eighth = A_WIDTHS[c] // 8
-        for q in range(8):
-            both = jnp.concatenate([a_in[c][q], a_in[c][8 + q]], axis=0)
-            first = A_STARTS[c] + q * eighth
-            a_out[:, first:first + eighth] = dot(put_a[...], both).astype(BF)
-        a_store(c).start()
-    for n in range(B_CHUNKS):
-        b_read(n).wait()
-        rows = dot(put_b, b_in[n].reshape(256, 2 * B_QUARTER)).astype(BF)
+        a_reads[c].wait()
+        columns = pl.ds(A_STARTS[c], A_WIDTHS[c])
+        both = jnp.concatenate([
+            jnp.concatenate([a_in[c][m * 8 + q] for q in range(8)], axis=1) for m in range(2)
+        ], axis=0)
+        a_out[:, columns] = dot(put_a[...], both).astype(BF)
+        stores.append(
+            pltpu.make_async_copy(a_out.at[:, columns], out_hbm.at[0, :, columns], a_sem.at[c])
+        )
+        stores[-1].start()
+    for read, (_, held, _, sem, start, width) in zip(reads, chunks):
+        read.wait()
+        quarter = width // 4
+        rows = dot(put_b, held[...].reshape(256, 2 * quarter)).astype(BF)
         for k in range(2):
             for g in range(4):
-                first = n * B_WIDTH + g * B_QUARTER
-                b_out[k, :, first:first + B_QUARTER] = rows[
-                    g * 64:(g + 1) * 64, k * B_QUARTER:(k + 1) * B_QUARTER
+                first = start + g * quarter
+                b_out[k, :, first:first + quarter] = rows[
+                    g * 64:(g + 1) * 64, k * quarter:(k + 1) * quarter
                 ]
-        b_store(n).start()
-    for c in range(A_CHUNKS):
-        a_store(c).wait()
-    for n in range(B_CHUNKS):
-        b_store(n).wait()
+        columns = pl.ds(start, width)
+        stores.append(
+            pltpu.make_async_copy(
+                b_out.at[:, :, columns], out_hbm.at[pl.ds(1, 2), :, columns], sem
+            )
+        )
+        stores[-1].start()
+    for copy in stores:
+        copy.wait()
 
 
 def on_device(gate_proj, up_proj, down_proj, rotation, placement, row_count):
     dma = pltpu.SemaphoreType.DMA
-    vmem = pl.BlockSpec(memory_space=pltpu.VMEM)
     smem = pl.BlockSpec(memory_space=pltpu.SMEM)
     hbm = pl.BlockSpec(memory_space=pl.ANY)
 
@@ -463,9 +548,13 @@
         return [held(*shape_of(w)) for w in A_WIDTHS]
 
     b = B_CHUNKS
+    c = C_CHUNKS
+    one = dma
+    each_a, each_b, each_c = dma((A_CHUNKS,)), dma((b,)), dma((c,))
     scratch = [
+        held(*gate_proj.shape), held(*up_proj.shape), held(*down_proj.shape),
         held(PIECE, HIDDEN), held(256, PIECE), held(512, PIECE),
-        held(2, 16, 16, PIECE), held(2, 16, 16, PIECE),
+        held(16, 2, 16, PIECE), held(16, 2, 16, PIECE),
         held(512, 256), held(64, 64), held(256, 128), held(512, 512),
         *per_a(lambda w: (128, w)),
         *per_a(lambda w: (128, w)),
@@ -476,24 +565,26 @@
         *per_a(lambda w: (16, 16, w // 8)),
         *per_a(lambda w: (16, 32, w // 8)),
         held(b, 256, B_WIDTH), held(b, 256, B_WIDTH), held(b, 256, B_WIDTH),
-        held(b, 2, 32, B_WIDTH), held(b, 2, 64, B_WIDTH),
-        held(b, 16, 16, 2 * B_QUARTER),
-        dma((A_CHUNKS,)), dma, dma, dma,
-        dma((A_CHUNKS,)), dma((A_CHUNKS,)), dma((A_CHUNKS,)), dma((A_CHUNKS,)), dma((A_CHUNKS,)),
-        dma((A_CHUNKS,)), dma((A_CHUNKS,)), dma((A_CHUNKS,)), dma((A_CHUNKS,)), dma((A_CHUNKS,)),
-        dma, dma((b,)), dma, dma((b,)), dma((b,)),
-        dma, dma, dma,
+        held(b, 2, 32, B_WIDTH), held(b, 2, 64, B_WIDTH), held(b, 16, 16, B_WIDTH // 2),
+        *[held(256, C_WIDTH)] * (3 * c),
+        *[held(2, 32, C_WIDTH)] * c, *[held(2, 64, C_WIDTH)] * c, *[held(16, 16, C_WIDTH // 2)] * c,
+        dma((3,)), each_a, one, one, one,
+        *[each_a] * 10,
+        one, each_b, one, each_b, each_b,
+        one, one, one,
+        *[each_c] * 8,
     ]
     arrived = [
         *(jax.ShapeDtypeStruct((16, 32, w // 8), BF) for w in A_WIDTHS),
-        jax.ShapeDtypeStruct((b, 16, 16, 2 * B_QUARTER), BF),
+        jax.ShapeDtypeStruct((b, 16, 16, B_WIDTH // 2), BF),
+        *[jax.ShapeDtypeStruct((16, 16, C_WIDTH // 2), BF)] * c,
         jax.ShapeDtypeStruct((64, 64), BF),
     ]
     limit = 60 * 1024 * 1024
     got = pl.pallas_call(
         kernel,
         out_shape=arrived,
-        in_specs=[smem, smem, vmem, vmem, vmem, hbm],
+        in_specs=[smem, smem, hbm, hbm, hbm, hbm],
         out_specs=[hbm] * len(arrived),
         scratch_shapes=scratch,
         compiler_params=pltpu.CompilerParams(
@@ -509,7 +600,7 @@
         scratch_shapes=[
             *(held(*v.shape) for v in arrived),
             held(64, HIDDEN), held(2, 64, HIDDEN),
-            dma((A_CHUNKS,)), dma((b,)), dma, dma((A_CHUNKS,)), dma((b,)),
+            one, each_a, each_b, each_c, each_a, each_b, each_c,
         ],
         compiler_params=pltpu.CompilerParams(vmem_limit_bytes=limit),
         name="place",

time: 75.8 us -> 75.8 us (level)
    pallas_call x1, Pallas kernels: 71.1 us -> 70.3 us  [on_device(): pl.pallas_call(kernel, out_shape=arrived, in_specs=[smem, smem, hbm, hbm,...]
where the time goes in v4:
time: 75.8 us; the launch traced here: 75.2 us
  Pallas kernels  75.2 us (99%)
    pallas_call x1, Pallas kernels, on_device(): pl.pallas_call(kernel, out_shape=arrived, in_specs=[smem, smem, hbm, hbm,...  70.3 us
    pallas_call x1, Pallas kernels, on_device(): pl.pallas_call(place_kernel, out_shape=jax.ShapeDtypeStruct((3, 64, HIDDE...  4.89 us

profile of v4, /device:TPU:0, one launch (start us, length us, event | category | flops | bytes accessed | tf_op | source)
XLA Modules:
  0.0 75.2 jit_solution(17473054713628022736)
XLA Ops:
  0.0 70.3 %rotate_and_send.1 = (bf16[16,32,128]{2,1,0:T(8,128)(2,1)}, bf16[16,32,256]{2,1,0:T(8,128)(2,1)}, bf16[16,32,256]{2,1,0:T(8,128)(2,1)}, bf16[16,32,256]{2,1,0:T(...) custom-call(s32[2,16]{1,0:T(2,128)} %placement_ref.1, ...), custom_call_target="tpu_custom_call" | custom-call | tf_op jit(solution)/shard_map/rotate_and_send/pallas_call | solution.py:584
  70.3 4.9 %place.1 = bf16[3,64,7168]{2,1,0:T(8,128)(2,1)} custom-call(bf16[16,32,128]{2,1,0:T(8,128)(2,1)} %get-tuple-element.13.refs_0_, bf16[16,32,256]{2,1,0:T(8,128)(2,1)} %get-tuple-element.14.refs_1_, bf16[16,32,256]{2,1,0:T(8,128)(2,1)} %get-tuple-element.15.refs_2_, bf16[16,32,256]{2,1,0:T(8,128)(2,1)} %get-tuple-element.16.refs_3_, ...), custom_call_target="tpu_custom_call" | custom-call | tf_op jit(solution)/shard_map/place/pallas_call | solution.py:595

commit v5 on v4

--- a/solution.py
+++ b/solution.py
@@ -105,6 +105,21 @@
     return onehot((slot == (r // 4) % 4) & (r % 4 == s // 32))
 
 
+def order_owner_rows():
+    r, s = iotas(256, 256)
+    return onehot(s == (r % 16) * 16 + ((r // 16) % 4) * 4 + r // 64)
+
+
+def place_rows(put_b, got, out):
+    width = got.shape[-1] // 2
+    rows = dot(put_b, got[...].reshape(256, 2 * width)).astype(BF)
+    for k in range(2):
+        for g in range(4):
+            out[k, :, g * width:(g + 1) * width] = rows[
+                g * 64:(g + 1) * 64, k * width:(k + 1) * width
+            ]
+
+
 def kernel(
     placement_ref, count_ref, gate_hbm, up_hbm, down_hbm, rot_hbm, *scratch
 ):
@@ -115,21 +130,22 @@
         del scratch[:count]
         return taken
 
-    a_got = take(A_CHUNKS)
-    b_got, *c_got = take(1 + C_CHUNKS)
-    (put_hbm,) = take(1)
+    part_hbm, last_got = take(2)
     gate, up, down = take(3)
-    rot, lhs_a, lhs_b, src, rcv, sel_a, put_a, sel_b, arrange = take(9)
-    a_core_out, a_core_in, a_own, a_far, a_near, a_sum, a_in, a_pick = (
-        take(A_CHUNKS) for _ in range(8)
+    rot, lhs_a, lhs_b, src, rcv, sel_a, put_a, sel_b, put_b, arrange = take(10)
+    a_core_out, a_core_in, a_own, a_far, a_near, a_sum, a_in, a_pick, a_got = (
+        take(A_CHUNKS) for _ in range(9)
     )
-    b_core_out, b_core_in, b_own, b_far, b_near, b_pick = take(6)
+    b_core_out, b_core_in, b_own, b_far, b_near, b_pick, b_got = take(7)
     c_core_out, c_core_in, c_own, c_far, c_near, c_pick = (take(C_CHUNKS) for _ in range(6))
-    in_sem, rot_sem, put_sem, src_send, src_recv = take(5)
+    c_got = take(C_CHUNKS - 1) + [last_got]
+    a_out, b_out, c_out = take(3)
+    in_sem, rot_sem, src_send, src_recv = take(4)
+    a_store_sem, b_store_sem, c_store_sem = take(3)
     a_core_send, a_core_recv, a_x_send, a_far_recv, a_near_recv = take(5)
-    a_in_send, a_in_recv, a_own_send, a_own_recv, a_self = take(5)
+    a_in_send, a_in_recv, a_own_send, a_own_recv = take(4)
     b_core_send, b_core_recv, b_x_send, b_far_recv, b_near_recv = take(5)
-    b_own_send, b_own_recv, b_self = take(3)
+    b_own_send, b_own_recv = take(2)
     c_core_send, c_core_recv, c_x_send, c_far_recv, c_near_recv = take(5)
     c_own_send, c_own_recv, c_self = take(3)
 
@@ -203,8 +219,8 @@
             hid, peers[i],
         )
 
-    def c_keep(n):
-        return pltpu.make_async_copy(c_pick[n].at[ep], c_got[n].at[ep], c_self.at[n])
+    def last_keep():
+        return pltpu.make_async_copy(c_pick[-1].at[ep], last_got.at[ep], c_self)
 
     def a_core(c):
         return remote(a_core_out[c], a_core_in[c], a_core_send.at[c], a_core_recv.at[c], other, ep)
@@ -225,18 +241,29 @@
             hid, peers[i],
         )
 
-    def a_keep(c):
-        return pltpu.make_async_copy(a_pick[c].at[ep], a_got[c].at[ep], a_self.at[c])
-
     def b_owner(n, i):
         return remote(
-            b_pick.at[n, peers[i]], b_got.at[n, ep], b_own_send, b_own_recv, hid, peers[i]
-        )
-
-    def b_keep(n):
-        return pltpu.make_async_copy(b_pick.at[n, ep], b_got.at[n, ep], b_self)
-
-    put_copy = pltpu.make_async_copy(put_a, put_hbm, put_sem)
+            b_pick.at[n, peers[i]], b_got.at[n, ep], b_own_send, b_own_recv.at[n], hid, peers[i]
+        )
+
+    def a_store(c):
+        columns = pl.ds(A_STARTS[c], A_WIDTHS[c])
+        return pltpu.make_async_copy(
+            a_out.at[:, columns], part_hbm.at[0, :, columns], a_store_sem.at[c]
+        )
+
+    def b_store(n):
+        columns = pl.ds(pl.multiple_of(n * B_WIDTH, B_WIDTH), B_WIDTH)
+        return pltpu.make_async_copy(
+            b_out.at[n], part_hbm.at[pl.ds(1, 2), :, columns], b_store_sem
+        )
+
+    def c_store(n):
+        columns = pl.ds(C_START + n * C_WIDTH, C_WIDTH)
+        return pltpu.make_async_copy(
+            c_out.at[n], part_hbm.at[pl.ds(1, 2), :, columns], c_store_sem.at[n]
+        )
+
     in_copies = [
         pltpu.make_async_copy(source, target, in_sem.at[i])
         for i, (source, target) in enumerate(((gate_hbm, gate), (up_hbm, up), (down_hbm, down)))
@@ -267,6 +294,8 @@
 
     def a_multiply(c):
         rot_copy(c).wait()
+        if c + 1 < A_CHUNKS:
+            rot_copy(c + 1).start()
 
         @pl.loop(0, A_WIDTHS[c] // TILE)
         def _(t):
@@ -303,7 +332,15 @@
         a_pick[c][...] = rows.astype(BF).reshape(16, 32, eighth)
         for i in range(OTHERS):
             a_owner(c, i).start()
-        a_keep(c).start()
+        a_got[c][ep] = a_pick[c][ep]
+
+    def a_place(c):
+        wait_bytes(a_got[c].at[pl.ds(0, OTHERS)], a_own_recv.at[c])
+        both = jnp.concatenate([
+            jnp.concatenate([a_got[c][m * 8 + q] for q in range(8)], axis=1) for m in range(2)
+        ], axis=0)
+        a_out[:, pl.ds(A_STARTS[c], A_WIDTHS[c])] = dot(put_a[...], both).astype(BF)
+        a_store(c).start()
 
     def multiply(width, start, core_out, own):
         total = dot(lhs_b[...], rot[:, pl.ds(start, width)])
@@ -338,7 +375,12 @@
         pick_rows(B_WIDTH, b_own.at[n], b_near.at[n], b_pick.at[n])
         for i in range(OTHERS):
             b_owner(n, i).start()
-        b_keep(n).start()
+        b_got[n, ep] = b_pick[n, ep]
+
+    def b_place(n):
+        wait_bytes(b_got.at[n, pl.ds(0, OTHERS)], b_own_recv.at[n])
+        place_rows(put_b[...], b_got.at[n], b_out.at[n])
+        b_store(n).start()
 
     def c_multiply(n):
         multiply(C_WIDTH, C_START + n * C_WIDTH, c_core_out[n], c_own[n])
@@ -356,12 +398,20 @@
         pick_rows(C_WIDTH, c_own[n], c_near[n], c_pick[n])
         for i in range(OTHERS):
             c_owner(n, i).start()
-        c_keep(n).start()
-
-    for copy in in_copies:
-        copy.start()
-    for c in range(A_CHUNKS):
-        rot_copy(c).start()
+        if n < C_CHUNKS - 1:
+            c_got[n][ep] = c_pick[n][ep]
+        else:
+            last_keep().start()
+
+    def c_place(n):
+        wait_bytes(c_got[n].at[pl.ds(0, OTHERS)], c_own_recv.at[n])
+        place_rows(put_b[...], c_got[n], c_out.at[n])
+        c_store(n).start()
+
+    in_copies[0].start()
+    rot_copy(0).start()
+    in_copies[1].start()
+    in_copies[2].start()
 
     r, s = iotas(256, 128)
     block = ((x + ring_offset((r // 32) % 4)) % 4) * 2 + jnp.where(r < 128, 1 - core, core)
@@ -371,6 +421,11 @@
     rows = sum(dot_t(onehot((expert == m) & (s == column)), gate[m]) for m in range(2))
     lhs_a[...] = rows.astype(BF)
 
+    a_multiply(0)
+
+    pl.semaphore_wait(barrier, 3 + OTHERS)
+
+    a_core(0).start()
     column = (r % 8) * 16 + r // 16
     expert = (r // 8) % 2
     spread = [onehot((expert == m) & (s == column)) for m in range(2)]
@@ -380,16 +435,11 @@
     in_copies[2].wait()
     rows = sum(dot(spread[m], down[m]) for m in range(2))
     src[:, 1] = rows.astype(BF).reshape(16, 16, PIECE)
-    a_multiply(0)
-
-    pl.semaphore_wait(barrier, 3 + OTHERS)
-
-    a_core(0).start()
     for i in range(OTHERS):
         src_copy(i).start()
+    a_sum_cores(0)
     a_multiply(1)
     a_core(1).start()
-    a_sum_cores(0)
     a_multiply(2)
     a_core(2).start()
     a_sum_cores(1)
@@ -410,7 +460,7 @@
         s == (r % 16) * 32 + ((r // 32) % 2) * 16 + ((r // 16) % 2) * 8 + block
     )
     put_a[...] = place_a(mine)
-    put_copy.start()
+    put_b[...] = order_owner_rows()
     sel_b[...] = select_b(low, high)
     a_to_peers(1)
     a_pass_on(3)
@@ -421,12 +471,16 @@
     a_to_owners(0)
     a_to_peers(2)
 
-    stages = ((b_sum_cores, 0), (b_multiply, -1), (b_pass_on, 1), (b_to_owners, 2))
+    stages = (
+        (b_sum_cores, 0), (b_multiply, -1), (b_pass_on, 1), (b_to_owners, 2), (b_place, 5),
+    )
     extras = {
         0: (lambda: a_to_owners(1), lambda: a_to_peers(3)),
         1: (lambda: a_to_owners(2),),
         2: (lambda: a_to_owners(3),),
-        B_CHUNKS - 1: (lambda: c_multiply(0),),
+        3: (lambda: a_place(0),),
+        4: (lambda: a_place(1),),
+        B_CHUNKS - 1: (lambda: c_multiply(0), lambda: c_multiply(1)),
     }
 
     @pl.loop(0, B_CHUNKS)
@@ -442,96 +496,71 @@
                     one()
 
     c_sum_cores(0)
-    c_multiply(1)
     b_pass_on(B_CHUNKS - 1)
+    c_sum_cores(1)
     b_to_owners(B_CHUNKS - 2)
-    c_sum_cores(1)
     c_pass_on(0)
     b_to_owners(B_CHUNKS - 1)
     c_pass_on(1)
+    a_place(2)
     c_to_owners(0)
+    a_place(3)
+    b_place(1)
     c_to_owners(1)
+    for n in range(2, B_CHUNKS):
+        b_place(n)
+    c_place(0)
 
     rest = pl.ds(0, OTHERS)
-    put_copy.wait()
     wait_bytes(src.at[rest], src_send)
     for c in range(A_CHUNKS):
         a_core(c).wait_send()
         wait_bytes(a_own[c].at[pl.ds(0, 96)], a_x_send.at[c])
         wait_bytes(a_sum[c].at[rest], a_in_send.at[c])
         wait_bytes(a_pick[c].at[rest], a_own_send.at[c])
-        a_keep(c).wait()
-        wait_bytes(a_got[c].at[rest], a_own_recv.at[c])
+        a_store(c).wait()
     wait_bytes(b_core_out, b_core_send)
     wait_bytes(b_own.at[:, pl.ds(0, 192)], b_x_send)
     wait_bytes(b_pick.at[:, rest], b_own_send)
-    wait_bytes(b_pick.at[:, 0], b_self)
-    wait_bytes(b_got.at[:, rest], b_own_recv)
     for n in range(C_CHUNKS):
         c_core(n).wait_send()
         wait_bytes(c_own[n].at[pl.ds(0, 192)], c_x_send.at[n])
         wait_bytes(c_pick[n].at[rest], c_own_send.at[n])
-        c_keep(n).wait()
-        wait_bytes(c_got[n].at[rest], c_own_recv.at[n])
-
-
-def place_kernel(*refs):
-    refs = list(refs)
-
-    def take(count):
-        taken = refs[:count]
-        del refs[:count]
-        return taken
-
-    a_got, (b_got,), c_got, (put_hbm, out_hbm) = take(A_CHUNKS), take(1), take(C_CHUNKS), take(2)
-    a_in, (b_in,), c_in, (put_a,) = take(A_CHUNKS), take(1), take(C_CHUNKS), take(1)
-    a_out, b_out, put_load, a_load, b_load, c_load, a_sem, b_sem, c_sem = refs
-
-    chunks = [
-        (b_got.at[n], b_in.at[n], b_load.at[n], b_sem.at[n], n * B_WIDTH, B_WIDTH)
-        for n in range(B_CHUNKS)
-    ] + [
-        (c_got[n], c_in[n], c_load.at[n], c_sem.at[n], C_START + n * C_WIDTH, C_WIDTH)
-        for n in range(C_CHUNKS)
+    last_keep().wait()
+    wait_bytes(b_out, b_store_sem)
+    c_store(0).wait()
+    wait_bytes(last_got.at[rest], c_own_recv.at[C_CHUNKS - 1])
+
+
+def place_kernel(part_hbm, last_got, out_hbm, got, held, load, got_load, store):
+    last = HIDDEN - C_WIDTH
+    pieces = [(pl.ds(0, 3), n * 1024, 1024) for n in range(last // 1024)]
+    pieces.append((pl.ds(0, 3), last - last % 1024, last % 1024))
+    pieces.append((pl.ds(0, 1), last, C_WIDTH))
+    pieces = [(kinds, slice(None), pl.ds(start, width)) for kinds, start, width in pieces]
+    loads = [
+        pltpu.make_async_copy(part_hbm.at[at], held.at[at], load.at[i])
+        for i, at in enumerate(pieces)
     ]
-    put_copy = pltpu.make_async_copy(put_hbm, put_a, put_load)
-    a_reads = [pltpu.make_async_copy(a_got[c], a_in[c], a_load.at[c]) for c in range(A_CHUNKS)]
-    reads = [pltpu.make_async_copy(got, held, load) for got, held, load, *_ in chunks]
-    stores = []
-    put_copy.start()
-    for copy in a_reads + reads:
+    pieces.append((pl.ds(1, 2), slice(None), pl.ds(last, C_WIDTH)))
+    stores = [
+        pltpu.make_async_copy(held.at[at], out_hbm.at[at], store.at[i])
+        for i, at in enumerate(pieces)
+    ]
+    got_copy = pltpu.make_async_copy(last_got, got, got_load)
+    got_copy.start()
+    for copy in loads:
         copy.start()
-    r, s = iotas(256, 256)
-    put_b = onehot(s == (r % 16) * 16 + ((r // 16) % 4) * 4 + r // 64)
-    put_copy.wait()
-    for c in range(A_CHUNKS):
-        a_reads[c].wait()
-        columns = pl.ds(A_STARTS[c], A_WIDTHS[c])
-        both = jnp.concatenate([
-            jnp.concatenate([a_in[c][m * 8 + q] for q in range(8)], axis=1) for m in range(2)
-        ], axis=0)
-        a_out[:, columns] = dot(put_a[...], both).astype(BF)
-        stores.append(
-            pltpu.make_async_copy(a_out.at[:, columns], out_hbm.at[0, :, columns], a_sem.at[c])
-        )
-        stores[-1].start()
-    for read, (_, held, _, sem, start, width) in zip(reads, chunks):
-        read.wait()
-        quarter = width // 4
-        rows = dot(put_b, held[...].reshape(256, 2 * quarter)).astype(BF)
-        for k in range(2):
-            for g in range(4):
-                first = start + g * quarter
-                b_out[k, :, first:first + quarter] = rows[
-                    g * 64:(g + 1) * 64, k * quarter:(k + 1) * quarter
-                ]
-        columns = pl.ds(start, width)
-        stores.append(
-            pltpu.make_async_copy(
-                b_out.at[:, :, columns], out_hbm.at[pl.ds(1, 2), :, columns], sem
-            )
-        )
-        stores[-1].start()
+    put_b = order_owner_rows()
+    for load, store in zip(loads[:4], stores[:4]):
+        load.wait()
+        store.start()
+    got_copy.wait()
+    place_rows(put_b, got, held.at[pl.ds(1, 2), :, pl.ds(last, C_WIDTH)])
+    stores[-1].start()
+    for load, store in zip(loads[4:], stores[4:]):
+        load.wait()
+        store.start()
     for copy in stores:
         copy.wait()
 
@@ -555,7 +584,7 @@
         held(*gate_proj.shape), held(*up_proj.shape), held(*down_proj.shape),
         held(PIECE, HIDDEN), held(256, PIECE), held(512, PIECE),
         held(16, 2, 16, PIECE), held(16, 2, 16, PIECE),
-        held(512, 256), held(64, 64), held(256, 128), held(512, 512),
+        held(512, 256), held(64, 64), held(256, 128), held(256, 256), held(512, 512),
         *per_a(lambda w: (128, w)),
         *per_a(lambda w: (128, w)),
         *per_a(lambda w: (128, w)),
@@ -564,47 +593,47 @@
         *per_a(lambda w: (16, 16, w // 8)),
         *per_a(lambda w: (16, 16, w // 8)),
         *per_a(lambda w: (16, 32, w // 8)),
+        *per_a(lambda w: (16, 32, w // 8)),
         held(b, 256, B_WIDTH), held(b, 256, B_WIDTH), held(b, 256, B_WIDTH),
-        held(b, 2, 32, B_WIDTH), held(b, 2, 64, B_WIDTH), held(b, 16, 16, B_WIDTH // 2),
+        held(b, 2, 32, B_WIDTH), held(b, 2, 64, B_WIDTH),
+        held(b, 16, 16, B_WIDTH // 2), held(b, 16, 16, B_WIDTH // 2),
         *[held(256, C_WIDTH)] * (3 * c),
         *[held(2, 32, C_WIDTH)] * c, *[held(2, 64, C_WIDTH)] * c, *[held(16, 16, C_WIDTH // 2)] * c,
-        dma((3,)), each_a, one, one, one,
-        *[each_a] * 10,
+        *[held(16, 16, C_WIDTH // 2)] * (c - 1),
+        held(64, HIDDEN), held(b, 2, 64, B_WIDTH), held(c, 2, 64, C_WIDTH),
+        dma((3,)), each_a, one, one,
+        each_a, one, each_c,
+        *[each_a] * 9,
         one, each_b, one, each_b, each_b,
-        one, one, one,
-        *[each_c] * 8,
+        one, each_b,
+        *[each_c] * 7, one,
     ]
     arrived = [
-        *(jax.ShapeDtypeStruct((16, 32, w // 8), BF) for w in A_WIDTHS),
-        jax.ShapeDtypeStruct((b, 16, 16, B_WIDTH // 2), BF),
-        *[jax.ShapeDtypeStruct((16, 16, C_WIDTH // 2), BF)] * c,
-        jax.ShapeDtypeStruct((64, 64), BF),
+        jax.ShapeDtypeStruct((3, 64, HIDDEN), BF),
+        jax.ShapeDtypeStruct((16, 16, C_WIDTH // 2), BF),
     ]
-    limit = 60 * 1024 * 1024
-    got = pl.pallas_call(
+    part, last_got = pl.pallas_call(
         kernel,
         out_shape=arrived,
         in_specs=[smem, smem, hbm, hbm, hbm, hbm],
         out_specs=[hbm] * len(arrived),
         scratch_shapes=scratch,
         compiler_params=pltpu.CompilerParams(
-            collective_id=0, has_side_effects=True, vmem_limit_bytes=limit
+            collective_id=0, has_side_effects=True, vmem_limit_bytes=56 * 1024 * 1024
         ),
         name="rotate_and_send",
     )(placement, row_count, gate_proj, up_proj, down_proj, rotation)
     out = pl.pallas_call(
         place_kernel,
         out_shape=jax.ShapeDtypeStruct((3, 64, HIDDEN), BF),
-        in_specs=[hbm] * len(got),
+        in_specs=[hbm] * 2,
         out_specs=hbm,
         scratch_shapes=[
-            *(held(*v.shape) for v in arrived),
-            held(64, HIDDEN), held(2, 64, HIDDEN),
-            one, each_a, each_b, each_c, each_a, each_b, each_c,
+            held(16, 16, C_WIDTH // 2), held(3, 64, HIDDEN), dma((9,)), one, dma((10,)),
         ],
-        compiler_params=pltpu.CompilerParams(vmem_limit_bytes=limit),
+        compiler_params=pltpu.CompilerParams(vmem_limit_bytes=60 * 1024 * 1024),
         name="place",
-    )(*got)
+    )(part, last_got)
     return jnp.transpose(out, (1, 0, 2))[None]
 
 

time: 75.8 us -> 74.2 us (0.979)
  Pallas kernels: 75.2 us -> 73.6 us
    pallas_call x1, Pallas kernels: 4.89 us -> 3.04 us  [on_device(): pl.pallas_call(place_kernel, out_shape=jax.ShapeDtypeStruct((3, 64, HIDDE...]
where the time goes in v5:
time: 74.2 us; the launch traced here: 73.6 us
  Pallas kernels  73.6 us (99%)
    pallas_call x1, Pallas kernels, on_device(): pl.pallas_call(kernel, out_shape=arrived, in_specs=[smem, smem, hbm, hbm,...  70.6 us
    pallas_call x1, Pallas kernels, on_device(): pl.pallas_call(place_kernel, out_shape=jax.ShapeDtypeStruct((3, 64, HIDDE...  3.04 us

profile of v5, /device:TPU:0, one launch (start us, length us, event | category | flops | bytes accessed | tf_op | source)
XLA Modules:
  0.0 73.6 jit_solution(15174890373119329611)
XLA Ops:
  0.0 70.6 %rotate_and_send.1 = (bf16[3,64,7168]{2,1,0:T(8,128)(2,1)}, bf16[16,16,256]{2,1,0:T(8,128)(2,1)}) custom-call(s32[2,16]{1,0:T(2,128)} %placement_ref.1, s32[2,16]{1,0:T(2,128)} %count_ref.1, bf16[2,896,128]{2,1,0:T(8,128)(2,1)} %gate_hbm.1, bf16[2,896,128]{2,1,0:T(8,128)(2,1)} %up_hbm.1, bf16[2,128,896]{2,1,0:T(8,128)(2,1)} %down_hbm.1, ...), custom_call_target="tpu_custom_call" | custom-call | tf_op jit(solution)/shard_map/rotate_and_send/pallas_call | solution.py:615
  70.6 3.0 %place.1 = bf16[3,64,7168]{2,1,0:T(8,128)(2,1)} custom-call(bf16[3,64,7168]{2,1,0:T(8,128)(2,1)} %get-tuple-element.7.part_hbm, bf16[16,16,256]{2,1,0:T(8,128)(2,1)} %get-tuple-element.8.last_got), custom_call_target="tpu_custom_call" | custom-call | tf_op jit(solution)/shard_map/place/pallas_call | solution.py:626

commit v6 on v5

--- a/solution.py
+++ b/solution.py
@@ -396,7 +396,7 @@
     def c_to_owners(n):
         wait_bytes(c_near[n], c_near_recv.at[n])
         pick_rows(C_WIDTH, c_own[n], c_near[n], c_pick[n])
-        for i in range(OTHERS):
+        for i in reversed(range(OTHERS)):
             c_owner(n, i).start()
         if n < C_CHUNKS - 1:
             c_got[n][ep] = c_pick[n][ep]
@@ -472,14 +472,12 @@
     a_to_peers(2)
 
     stages = (
-        (b_sum_cores, 0), (b_multiply, -1), (b_pass_on, 1), (b_to_owners, 2), (b_place, 5),
+        (b_sum_cores, 0), (b_multiply, -1), (b_pass_on, 1), (b_to_owners, 2),
     )
     extras = {
         0: (lambda: a_to_owners(1), lambda: a_to_peers(3)),
         1: (lambda: a_to_owners(2),),
         2: (lambda: a_to_owners(3),),
-        3: (lambda: a_place(0),),
-        4: (lambda: a_place(1),),
         B_CHUNKS - 1: (lambda: c_multiply(0), lambda: c_multiply(1)),
     }
 
@@ -498,16 +496,20 @@
     c_sum_cores(0)
     b_pass_on(B_CHUNKS - 1)
     c_sum_cores(1)
+    a_place(0)
+    a_place(1)
     b_to_owners(B_CHUNKS - 2)
     c_pass_on(0)
+    a_place(2)
+    a_place(3)
     b_to_owners(B_CHUNKS - 1)
     c_pass_on(1)
-    a_place(2)
+    b_place(0)
+    b_place(1)
     c_to_owners(0)
-    a_place(3)
-    b_place(1)
+    b_place(2)
     c_to_owners(1)
-    for n in range(2, B_CHUNKS):
+    for n in range(3, B_CHUNKS):
         b_place(n)
     c_place(0)
 

time: 74.2 us -> 74.2 us (level)
  no operation moved by 1% of the time
where the time goes in v6:
time: 74.2 us; the launch traced here: 73.3 us
  Pallas kernels  73.3 us (99%)
    pallas_call x1, Pallas kernels, on_device(): pl.pallas_call(kernel, out_shape=arrived, in_specs=[smem, smem, hbm, hbm,...  70.2 us
    pallas_call x1, Pallas kernels, on_device(): pl.pallas_call(place_kernel, out_shape=jax.ShapeDtypeStruct((3, 64, HIDDE...  3.05 us

profile of v6, /device:TPU:0, one launch (start us, length us, event | category | flops | bytes accessed | tf_op | source)
XLA Modules:
  0.0 73.3 jit_solution(5467942871883366877)
XLA Ops:
  0.0 70.2 %rotate_and_send.1 = (bf16[3,64,7168]{2,1,0:T(8,128)(2,1)}, bf16[16,16,256]{2,1,0:T(8,128)(2,1)}) custom-call(s32[2,16]{1,0:T(2,128)} %placement_ref.1, s32[2,16]{1,0:T(2,128)} %count_ref.1, bf16[2,896,128]{2,1,0:T(8,128)(2,1)} %gate_hbm.1, bf16[2,896,128]{2,1,0:T(8,128)(2,1)} %up_hbm.1, bf16[2,128,896]{2,1,0:T(8,128)(2,1)} %down_hbm.1, ...), custom_call_target="tpu_custom_call" | custom-call | tf_op jit(solution)/shard_map/rotate_and_send/pallas_call | solution.py:617
  70.2 3.0 %place.1 = bf16[3,64,7168]{2,1,0:T(8,128)(2,1)} custom-call(bf16[3,64,7168]{2,1,0:T(8,128)(2,1)} %get-tuple-element.7.part_hbm, bf16[16,16,256]{2,1,0:T(8,128)(2,1)} %get-tuple-element.8.last_got), custom_call_target="tpu_custom_call" | custom-call | tf_op jit(solution)/shard_map/place/pallas_call | solution.py:628

commit v7 on v6

--- a/solution.py
+++ b/solution.py
@@ -472,7 +472,7 @@
     a_to_peers(2)
 
     stages = (
-        (b_sum_cores, 0), (b_multiply, -1), (b_pass_on, 1), (b_to_owners, 2),
+        (b_sum_cores, 0), (b_pass_on, 1), (b_multiply, -1), (b_to_owners, 2),
     )
     extras = {
         0: (lambda: a_to_owners(1), lambda: a_to_peers(3)),

time: 74.2 us -> 74.2 us (level)
  no operation moved by 1% of the time
where the time goes in v7:
time: 74.2 us; the launch traced here: 73.2 us
  Pallas kernels  73.2 us (99%)
    pallas_call x1, Pallas kernels, on_device(): pl.pallas_call(kernel, out_shape=arrived, in_specs=[smem, smem, hbm, hbm,...  70.2 us
    pallas_call x1, Pallas kernels, on_device(): pl.pallas_call(place_kernel, out_shape=jax.ShapeDtypeStruct((3, 64, HIDDE...  3.05 us

profile of v7, /device:TPU:0, one launch (start us, length us, event | category | flops | bytes accessed | tf_op | source)
XLA Modules:
  0.0 73.2 jit_solution(3704397230264010419)
XLA Ops:
  0.0 70.2 %rotate_and_send.1 = (bf16[3,64,7168]{2,1,0:T(8,128)(2,1)}, bf16[16,16,256]{2,1,0:T(8,128)(2,1)}) custom-call(s32[2,16]{1,0:T(2,128)} %placement_ref.1, s32[2,16]{1,0:T(2,128)} %count_ref.1, bf16[2,896,128]{2,1,0:T(8,128)(2,1)} %gate_hbm.1, bf16[2,896,128]{2,1,0:T(8,128)(2,1)} %up_hbm.1, bf16[2,128,896]{2,1,0:T(8,128)(2,1)} %down_hbm.1, ...), custom_call_target="tpu_custom_call" | custom-call | tf_op jit(solution)/shard_map/rotate_and_send/pallas_call | solution.py:617
  70.2 3.0 %place.1 = bf16[3,64,7168]{2,1,0:T(8,128)(2,1)} custom-call(bf16[3,64,7168]{2,1,0:T(8,128)(2,1)} %get-tuple-element.7.part_hbm, bf16[16,16,256]{2,1,0:T(8,128)(2,1)} %get-tuple-element.8.last_got), custom_call_target="tpu_custom_call" | custom-call | tf_op jit(solution)/shard_map/place/pallas_call | solution.py:628
